TPU v7x, 32 devices: a whole 2x2x4 slice. The times are simulated.
32 devices in a mesh: dp: 4 (over y, x), seq: 8 (over z, core).
Axes of the slice: x: 2, y: 2, z: 4, core: 2. Of those that a mesh axis runs over, the one named last changes fastest.
Arguments:
- tokens: bfloat16 [8, 1024, 1024], P('dp', 'seq'), may hold values from -6 to 6
- memory: bfloat16 [8, 128, 1024], P('dp', 'seq'), may hold values from -6 to 6
- lengths: int32 [8, 8], P('dp'), may hold values from 1 to 1017, as said below
- memory_segments: int32 [8, 128], P('dp'), may hold values from 0 to 7, never falling along the last dimension, each value on 1 to 64 neighbouring positions
- out_grad: bfloat16 [8, 1024, 1024], P('dp', 'seq'), may hold values from -6 to 6
- self_query: bfloat16 [1024, 1024], P(('dp', 'seq')), may hold values from -0.1875 to 0.1875
- self_key: bfloat16 [1024, 1024], P(('dp', 'seq')), may hold values from -0.1875 to 0.1875
- self_value: bfloat16 [1024, 1024], P(('dp', 'seq')), may hold values from -0.1875 to 0.1875
- self_out: bfloat16 [1024, 1024], P(('dp', 'seq')), may hold values from -6 to 6
- cross_query: bfloat16 [1024, 1024], P(('dp', 'seq')), may hold values from -0.1875 to 0.1875
- cross_key: bfloat16 [1024, 1024], P(('dp', 'seq')), may hold values from -0.1875 to 0.1875
- cross_value: bfloat16 [1024, 1024], P(('dp', 'seq')), may hold values from -0.1875 to 0.1875
- cross_out: bfloat16 [1024, 1024], P(('dp', 'seq')), may hold values from -6 to 6
- expand_weight: bfloat16 [1024, 4096], P(('dp', 'seq')), may hold values from -0.1875 to 0.1875
- shrink_weight: bfloat16 [4096, 1024], P(('dp', 'seq')), may hold values from -0.5 to 0.5
- norm_gains: bfloat16 [3, 1024], P(None, ('dp', 'seq')), may hold values from 0.5 to 1.5
- norm_biases: bfloat16 [3, 1024], P(None, ('dp', 'seq')), may hold values from -1.75 to 1.75
Outputs:
- output: bfloat16 [8, 1024, 1024], P('dp', 'seq')
- input_grad: float32 [8, 1024, 1024], P('dp', 'seq')
- memory_grad: float32 [8, 128, 1024], P('dp', 'seq')
- self_query_grad: float32 [1024, 1024], P(('dp', 'seq'))
- self_key_grad: float32 [1024, 1024], P(('dp', 'seq'))
- self_value_grad: float32 [1024, 1024], P(('dp', 'seq'))
- self_out_grad: float32 [1024, 1024], P(('dp', 'seq'))
- cross_query_grad: float32 [1024, 1024], P(('dp', 'seq'))
- cross_key_grad: float32 [1024, 1024], P(('dp', 'seq'))
- cross_value_grad: float32 [1024, 1024], P(('dp', 'seq'))
- cross_out_grad: float32 [1024, 1024], P(('dp', 'seq'))
- expand_grad: float32 [1024, 4096], P(('dp', 'seq'))
- shrink_grad: float32 [4096, 1024], P(('dp', 'seq'))
- gains_grad: float32 [3, 1024], P(None, ('dp', 'seq'))
- biases_grad: float32 [3, 1024], P(None, ('dp', 'seq'))
Inputs may be any that keep to these rules, and one draw needn't show every extreme that they name: `lengths`: each row gives the token counts of the 8 sentences of a stream, which fill its 1024 tokens in order. In all streams but one, every sentence has 32 to 256 tokens; in one stream a single sentence takes all tokens but one at each side of it and at the end. `memory_segments`: each row gives, in order, the sentence of each memory position of a stream; every sentence has some positions.
All inputs are finite; a program needn't handle non-finite values.
Results may differ from a plain program's by a relative error of at most 0.022.
Values may be sent and summed in bfloat16 or wider, within the bound.
A program may use at most 256 MiB of HBM per device.

v0:
```python
import jax
import jax.numpy as jnp
from jax import lax
from jax.sharding import PartitionSpec as P

H = 16
HD = 64
MB = 2


alpha_scale = 300.0**0.25
norm_eps = 1e-05
masked_score = -1e30


def layer_norm(value, gain, bias):
    average = jnp.mean(value, axis=-1, keepdims=True)
    centred = value - average
    spread = jnp.mean(centred * centred, axis=-1, keepdims=True)
    return centred * lax.rsqrt(spread + norm_eps) * gain + bias


def project(left, right):
    return jnp.dot(left, right, preferred_element_type=jnp.float32)


def project_back(left, right):
    return lax.dot_general(
        left, right, (((1,), (1,)), ((), ())), preferred_element_type=jnp.float32
    )


def weight_term(left, right):
    return lax.dot_general(
        left, right, (((0,), (0,)), ((), ())), preferred_element_type=jnp.float32
    )


def split_heads(value):
    return value.reshape(value.shape[0], value.shape[1], H, HD)


def sentence_ids(sent_ends, places):
    return jnp.sum((places[None, :, None] >= sent_ends[:, None, :]).astype(jnp.int32), axis=2)


def masked_scores(queries, key_heads, allowed, scaling):
    raw_scores = (
        jnp.einsum("gqhd,gkhd->ghqk", queries, key_heads, preferred_element_type=jnp.float32)
        * scaling
    )
    return jnp.where(allowed[:, None], raw_scores, masked_score)


def attend_forward(queries, key_heads, value_heads, allowed, scaling):
    scores = masked_scores(queries, key_heads, allowed, scaling)
    row_max = jnp.max(scores, axis=3, keepdims=True)
    powers = jnp.exp(scores - row_max)
    row_total = jnp.sum(powers, axis=3, keepdims=True)
    prob_low = (powers / row_total).astype(jnp.bfloat16)
    attended = jnp.einsum(
        "ghqk,gkhd->gqhd", prob_low, value_heads, preferred_element_type=jnp.float32
    )
    return (attended, row_max + jnp.log(row_total))


def attend_backward(queries, key_heads, value_heads, allowed, scaling, log_total, attended_grad):
    scores = masked_scores(queries, key_heads, allowed, scaling)
    probability = jnp.exp(scores - log_total)
    prob_grad = jnp.einsum(
        "gqhd,gkhd->ghqk", attended_grad, value_heads, preferred_element_type=jnp.float32
    )
    score_grad = probability * (prob_grad - jnp.sum(prob_grad * probability, axis=3, keepdims=True))
    score_low = score_grad.astype(jnp.bfloat16)
    query_grad = (
        jnp.einsum("ghqk,gkhd->gqhd", score_low, key_heads, preferred_element_type=jnp.float32)
        * scaling
    )
    return (query_grad, score_low, probability.astype(jnp.bfloat16))


def micro_batch(gathered, tokens, memory, lengths, memory_segments, out_grad):
    (
        self_query,
        self_key,
        self_value,
        self_out,
        cross_query,
        cross_key,
        cross_value,
        cross_out,
        expand_weight,
        shrink_weight,
        norm_gains,
        norm_biases,
    ) = gathered
    gains = norm_gains.astype(jnp.float32)
    biases = norm_biases.astype(jnp.float32)
    group_size, local_len, features = tokens.shape
    seq_count = lax.axis_size("seq")
    seq_index = lax.axis_index("seq")
    full_len = local_len * seq_count
    row_count = group_size * local_len
    scaling = HD ** (-0.5)
    sent_ends = jnp.cumsum(lengths, axis=1)[:, :-1]
    query_places = seq_index * local_len + jnp.arange(local_len, dtype=jnp.int32)
    key_places = jnp.arange(full_len, dtype=jnp.int32)
    query_ids = sentence_ids(sent_ends, query_places)
    key_ids = sentence_ids(sent_ends, key_places)
    self_allowed = (query_ids[:, :, None] == key_ids[:, None, :]) & (
        key_places[None, None, :] <= query_places[None, :, None]
    )
    cross_allowed = query_ids[:, :, None] == memory_segments[:, None, :]
    token_rows = tokens.reshape(row_count, features)
    queries = split_heads(
        project(token_rows, self_query)
        .astype(jnp.bfloat16)
        .reshape(group_size, local_len, features)
    )
    own_keys = (
        project(token_rows, self_key).astype(jnp.bfloat16).reshape(group_size, local_len, features)
    )
    own_values = (
        project(token_rows, self_value)
        .astype(jnp.bfloat16)
        .reshape(group_size, local_len, features)
    )
    all_keys, all_values = (
        lax.all_gather(own_keys, "seq", axis=1, tiled=True),
        lax.all_gather(own_values, "seq", axis=1, tiled=True),
    )
    key_heads = split_heads(all_keys)
    value_heads = split_heads(all_values)
    attended, self_log = attend_forward(queries, key_heads, value_heads, self_allowed, scaling)
    attended = attended.reshape(row_count, features).astype(jnp.bfloat16)
    first_pre = alpha_scale * token_rows.astype(jnp.float32) + project(attended, self_out)
    first, first_pull = jax.vjp(layer_norm, first_pre, gains[0], biases[0])
    first_low = first.astype(jnp.bfloat16)
    cross_queries = split_heads(
        project(first_low, cross_query)
        .astype(jnp.bfloat16)
        .reshape(group_size, local_len, features)
    )
    own_memory = memory.reshape(-1, features)
    memory_all = lax.all_gather(memory, "seq", axis=1, tiled=True)
    memory_rows = memory_all.reshape(-1, features)
    cross_keys = (
        project(memory_rows, cross_key).astype(jnp.bfloat16).reshape(group_size, -1, features)
    )
    cross_values = (
        project(memory_rows, cross_value).astype(jnp.bfloat16).reshape(group_size, -1, features)
    )
    cross_key_heads = split_heads(cross_keys)
    cross_value_heads = split_heads(cross_values)
    cross_attended, cross_log = attend_forward(
        cross_queries, cross_key_heads, cross_value_heads, cross_allowed, scaling
    )
    cross_attended = cross_attended.reshape(row_count, features).astype(jnp.bfloat16)
    second_pre = alpha_scale * first + project(cross_attended, cross_out)
    second, second_pull = jax.vjp(layer_norm, second_pre, gains[1], biases[1])
    second_low = second.astype(jnp.bfloat16)
    upward = project(second_low, expand_weight)
    active, gelu_pull = jax.vjp(jax.nn.gelu, upward)
    active_low = active.astype(jnp.bfloat16)
    third_pre = alpha_scale * second + project(active_low, shrink_weight)
    final, third_pull = jax.vjp(layer_norm, third_pre, gains[2], biases[2])
    third_grad, gain_third, bias_third = third_pull(
        out_grad.reshape(row_count, features).astype(jnp.float32)
    )
    branch_grad = third_grad.astype(jnp.bfloat16)
    shrink_grad = weight_term(active_low, branch_grad)
    (up_grad,) = gelu_pull(project_back(branch_grad, shrink_weight))
    up_low = up_grad.astype(jnp.bfloat16)
    expand_grad = weight_term(second_low, up_low)
    second_grad = alpha_scale * third_grad + project_back(up_low, expand_weight)
    second_pre_grad, gain_second, bias_second = second_pull(second_grad)
    cross_branch = second_pre_grad.astype(jnp.bfloat16)
    cross_out_grad = weight_term(cross_attended, cross_branch)
    cross_attended_grad = split_heads(
        project_back(cross_branch, cross_out)
        .astype(jnp.bfloat16)
        .reshape(group_size, local_len, features)
    )
    cross_q_grad, cross_scores, cross_probs = attend_backward(
        cross_queries,
        cross_key_heads,
        cross_value_heads,
        cross_allowed,
        scaling,
        cross_log,
        cross_attended_grad,
    )
    cross_q_low = cross_q_grad.reshape(row_count, features).astype(jnp.bfloat16)
    cross_query_grad = weight_term(first_low, cross_q_low)
    key_term = (
        jnp.einsum(
            "ghqk,gqhd->gkhd", cross_scores, cross_queries, preferred_element_type=jnp.float32
        )
        * scaling
    ).reshape(group_size, -1, features)
    value_term = jnp.einsum(
        "ghqk,gqhd->gkhd", cross_probs, cross_attended_grad, preferred_element_type=jnp.float32
    ).reshape(group_size, -1, features)
    key_summed, value_summed = (
        lax.psum_scatter(
            key_term.astype(jnp.bfloat16), "seq", scatter_dimension=1, tiled=True
        ).astype(jnp.float32),
        lax.psum_scatter(
            value_term.astype(jnp.bfloat16), "seq", scatter_dimension=1, tiled=True
        ).astype(jnp.float32),
    )
    key_low = key_summed.reshape(-1, features).astype(jnp.bfloat16)
    value_low = value_summed.reshape(-1, features).astype(jnp.bfloat16)
    cross_key_grad = weight_term(own_memory, key_low)
    cross_value_grad = weight_term(own_memory, value_low)
    memory_grad = (project_back(key_low, cross_key) + project_back(value_low, cross_value)).reshape(
        memory.shape
    )
    first_grad = alpha_scale * second_pre_grad + project_back(cross_q_low, cross_query)
    first_pre_grad, gain_first, bias_first = first_pull(first_grad)
    self_branch = first_pre_grad.astype(jnp.bfloat16)
    self_out_grad = weight_term(attended, self_branch)
    attended_grad = split_heads(
        project_back(self_branch, self_out)
        .astype(jnp.bfloat16)
        .reshape(group_size, local_len, features)
    )
    self_q_grad, self_scores, self_probs = attend_backward(
        queries, key_heads, value_heads, self_allowed, scaling, self_log, attended_grad
    )
    count = local_len * lax.axis_size("seq")
    key_part = (
        jnp.einsum("ghqk,gqhd->kghd", self_scores, queries, preferred_element_type=jnp.float32)
        * scaling
    )
    value_part = jnp.einsum(
        "ghqk,gqhd->kghd", self_probs, attended_grad, preferred_element_type=jnp.float32
    )
    pair_summed = lax.psum_scatter(
        jnp.concatenate(
            [
                key_part.reshape(count, group_size, features),
                value_part.reshape(count, group_size, features),
            ],
            axis=2,
        ).astype(jnp.bfloat16),
        "seq",
        scatter_dimension=0,
        tiled=True,
    ).astype(jnp.float32)
    key_grad = (
        pair_summed[:, :, :features]
        .astype(jnp.bfloat16)
        .transpose(1, 0, 2)
        .reshape(row_count, features)
    )
    value_grad = (
        pair_summed[:, :, features:]
        .astype(jnp.bfloat16)
        .transpose(1, 0, 2)
        .reshape(row_count, features)
    )
    query_low = self_q_grad.reshape(row_count, features).astype(jnp.bfloat16)
    self_query_grad = weight_term(token_rows, query_low)
    self_key_grad = weight_term(token_rows, key_grad)
    self_value_grad = weight_term(token_rows, value_grad)
    input_grad = (
        alpha_scale * first_pre_grad
        + project_back(query_low, self_query)
        + project_back(key_grad, self_key)
        + project_back(value_grad, self_value)
    )
    gains_grad = jnp.stack([gain_first, gain_second, gain_third])
    biases_grad = jnp.stack([bias_first, bias_second, bias_third])
    gradients = (
        self_query_grad,
        self_key_grad,
        self_value_grad,
        self_out_grad,
        cross_query_grad,
        cross_key_grad,
        cross_value_grad,
        cross_out_grad,
        expand_grad,
        shrink_grad,
        gains_grad,
        biases_grad,
    )
    result = final.astype(jnp.bfloat16).reshape(group_size, local_len, features)
    return (result, input_grad.reshape(group_size, local_len, features), memory_grad, gradients)


def shards(
    tokens,
    memory,
    lengths,
    memory_segments,
    out_grad,
    self_query,
    self_key,
    self_value,
    self_out,
    cross_query,
    cross_key,
    cross_value,
    cross_out,
    expand_weight,
    shrink_weight,
    norm_gains,
    norm_biases,
):
    group_size = tokens.shape[0] // MB
    outputs = []
    input_grads = []
    memory_grads = []
    totals = None
    for batch_index in range(MB):
        gathered = (
            lax.all_gather(self_query, ("dp", "seq"), axis=0, tiled=True),
            lax.all_gather(self_key, ("dp", "seq"), axis=0, tiled=True),
            lax.all_gather(self_value, ("dp", "seq"), axis=0, tiled=True),
            lax.all_gather(self_out, ("dp", "seq"), axis=0, tiled=True),
            lax.all_gather(cross_query, ("dp", "seq"), axis=0, tiled=True),
            lax.all_gather(cross_key, ("dp", "seq"), axis=0, tiled=True),
            lax.all_gather(cross_value, ("dp", "seq"), axis=0, tiled=True),
            lax.all_gather(cross_out, ("dp", "seq"), axis=0, tiled=True),
            lax.all_gather(expand_weight, ("dp", "seq"), axis=0, tiled=True),
            lax.all_gather(shrink_weight, ("dp", "seq"), axis=0, tiled=True),
            lax.all_gather(norm_gains, ("dp", "seq"), axis=1, tiled=True),
            lax.all_gather(norm_biases, ("dp", "seq"), axis=1, tiled=True),
        )
        start = batch_index * group_size
        stop = start + group_size
        result, input_grad, memory_grad, gradients = micro_batch(
            gathered,
            tokens[start:stop],
            memory[start:stop],
            lengths[start:stop],
            memory_segments[start:stop],
            out_grad[start:stop],
        )
        outputs.append(result)
        input_grads.append(input_grad)
        memory_grads.append(memory_grad)
        if totals is None:
            totals = gradients
        else:
            totals = tuple((running + gradient for running, gradient in zip(totals, gradients)))
    summed = (
        lax.psum_scatter(totals[0], ("dp", "seq"), scatter_dimension=0, tiled=True),
        lax.psum_scatter(totals[1], ("dp", "seq"), scatter_dimension=0, tiled=True),
        lax.psum_scatter(totals[2], ("dp", "seq"), scatter_dimension=0, tiled=True),
        lax.psum_scatter(totals[3], ("dp", "seq"), scatter_dimension=0, tiled=True),
        lax.psum_scatter(totals[4], ("dp", "seq"), scatter_dimension=0, tiled=True),
        lax.psum_scatter(totals[5], ("dp", "seq"), scatter_dimension=0, tiled=True),
        lax.psum_scatter(totals[6], ("dp", "seq"), scatter_dimension=0, tiled=True),
        lax.psum_scatter(totals[7], ("dp", "seq"), scatter_dimension=0, tiled=True),
        lax.psum_scatter(totals[8], ("dp", "seq"), scatter_dimension=0, tiled=True),
        lax.psum_scatter(totals[9], ("dp", "seq"), scatter_dimension=0, tiled=True),
        lax.psum_scatter(totals[10], ("dp", "seq"), scatter_dimension=1, tiled=True),
        lax.psum_scatter(totals[11], ("dp", "seq"), scatter_dimension=1, tiled=True),
    )
    return (
        jnp.concatenate(outputs, 0),
        jnp.concatenate(input_grads, 0),
        jnp.concatenate(memory_grads, 0),
        summed[0],
        summed[1],
        summed[2],
        summed[3],
        summed[4],
        summed[5],
        summed[6],
        summed[7],
        summed[8],
        summed[9],
        summed[10],
        summed[11],
    )


def solution(mesh):
    return jax.shard_map(
        shards,
        mesh=mesh,
        in_specs=(
            P("dp", "seq", None),
            P("dp", "seq", None),
            P("dp", None),
            P("dp", None),
            P("dp", "seq", None),
            P(("dp", "seq"), None),
            P(("dp", "seq"), None),
            P(("dp", "seq"), None),
            P(("dp", "seq"), None),
            P(("dp", "seq"), None),
            P(("dp", "seq"), None),
            P(("dp", "seq"), None),
            P(("dp", "seq"), None),
            P(("dp", "seq"), None),
            P(("dp", "seq"), None),
            P(None, ("dp", "seq")),
            P(None, ("dp", "seq")),
        ),
        out_specs=(
            P("dp", "seq", None),
            P("dp", "seq", None),
            P("dp", "seq", None),
            P(("dp", "seq"), None),
            P(("dp", "seq"), None),
            P(("dp", "seq"), None),
            P(("dp", "seq"), None),
            P(("dp", "seq"), None),
            P(("dp", "seq"), None),
            P(("dp", "seq"), None),
            P(("dp", "seq"), None),
            P(("dp", "seq"), None),
            P(("dp", "seq"), None),
            P(None, ("dp", "seq")),
            P(None, ("dp", "seq")),
        ),
        check_vma=False,
    )
```

profile of v0, /device:TPU:0, one launch (start us, length us, event | category | flops | bytes accessed | tf_op | source)
XLA Modules:
  0.0 2796.0 jit_solution(4830065569732981495)
XLA Ops:
  10.6 59.6 %all-gather.21.cloned.1.call-done = bf16[1024,1024]{1,0:T(8,128)(2,1)} async-done(((bf16[32,1024]{1,0:T(8,128)(2,1)}), bf16[1024,1024]{1,0:T(8,128)(2,1)}) %all-gather.21.cloned.1.call-update) | async-done | bytes 2097168 | tf_op jit(solution)/shard_map/all_gather | solution.py:321
  73.1 55.4 %all-gather.25.cloned.1.call-done = bf16[1024,1024]{1,0:T(8,128)(2,1)} async-done(((bf16[32,1024]{1,0:T(8,128)(2,1)}), bf16[1024,1024]{1,0:T(8,128)(2,1)}) %all-gather.25.cloned.1.call-update) | async-done | bytes 2097168 | tf_op jit(solution)/shard_map/all_gather | solution.py:320
  139.3 39.4 %all-gather.4 = bf16[32,32,3]{1,2,0:T(4,128)(2,1)S(1)} all-gather(bf16[1,32,3]{1,2,0:T(4,128)(2,1)S(1)} %bitcast.509), channel_id=1, replica_groups=mesh['dp'=4,'seq'=8] {'dp','seq'}, dimensions={0}, use_global_device_ids=true | all-gather | bytes 6336 | tf_op jit(solution)/shard_map/all_gather | solution.py:329
  178.8 36.7 %all-gather.5 = bf16[32,32,3]{1,2,0:T(4,128)(2,1)S(1)} all-gather(bf16[1,32,3]{1,2,0:T(4,128)(2,1)S(1)} %bitcast.510), channel_id=1, replica_groups=mesh['dp'=4,'seq'=8] {'dp','seq'}, dimensions={0}, use_global_device_ids=true | all-gather | bytes 6336 | tf_op jit(solution)/shard_map/all_gather | solution.py:330
  215.8 14.5 all_gather.74
  230.3 14.5 all_gather.83
  258.9 45.0 %all-gather.23.cloned.1.call-done = bf16[1024,1024]{1,0:T(8,128)(2,1)} async-done(((bf16[32,1024]{1,0:T(8,128)(2,1)}), bf16[1024,1024]{1,0:T(8,128)(2,1)}) %all-gather.23.cloned.1.call-update) | async-done | bytes 2097168 | tf_op jit(solution)/shard_map/all_gather | solution.py:319
  308.5 25.3 all-gather.41.cloned.1.call-done
  338.3 26.4 all-gather.43.cloned.1.call-done
  376.1 47.6 %all-gather.27.cloned.1.call-done = bf16[1024,1024]{1,0:T(8,128)(2,1)} async-done(((bf16[32,1024]{1,0:T(8,128)(2,1)}), bf16[1024,1024]{1,0:T(8,128)(2,1)}) %all-gather.27.cloned.1.call-update) | async-done | bytes 2097168 | tf_op jit(solution)/shard_map/all_gather | solution.py:322
  426.1 56.0 %all-gather.31.cloned.1.call-done = bf16[1024,1024]{1,0:T(8,128)(2,1)} async-done(((bf16[32,1024]{1,0:T(8,128)(2,1)}), bf16[1024,1024]{1,0:T(8,128)(2,1)}) %all-gather.31.cloned.1.call-update) | async-done | bytes 2097168 | tf_op jit(solution)/shard_map/all_gather | solution.py:323
  485.0 27.0 all-gather.45.cloned.1.call-done
  516.0 26.3 all-gather.47.cloned.1.call-done
  560.9 40.2 %all-gather.35.cloned.1.call-done = bf16[1024,1024]{1,0:T(8,128)(2,1)} async-done(((bf16[32,1024]{1,0:T(8,128)(2,1)}), bf16[1024,1024]{1,0:T(8,128)(2,1)}) %all-gather.35.cloned.1.call-update) | async-done | bytes 2097168 | tf_op jit(solution)/shard_map/all_gather | solution.py:326
  607.2 73.1 %all-gather.37.cloned.1.call-done = bf16[1024,4096]{1,0:T(8,128)(2,1)} async-done(((bf16[32,4096]{1,0:T(8,128)(2,1)}), bf16[1024,4096]{1,0:T(8,128)(2,1)}) %all-gather.37.cloned.1.call-update) | async-done | bytes 8388624 | tf_op jit(solution)/shard_map/all_gather | solution.py:327
  686.7 72.5 %all-gather.39.cloned.1.call-done = bf16[4096,1024]{1,0:T(8,128)(2,1)} async-done(((bf16[128,1024]{1,0:T(8,128)(2,1)}), bf16[4096,1024]{1,0:T(8,128)(2,1)}) %all-gather.39.cloned.1.call-update) | async-done | bytes 8388624 | tf_op jit(solution)/shard_map/all_gather | solution.py:328
  835.4 8.9 multiply_convert_fusion.1
  943.0 17.2 reduce-scatter.43.cloned.1.call-done
  961.5 49.0 %reduce-scatter.45.cloned.1.call-done = bf16[128,2048]{1,0:T(8,128)(2,1)} async-done(((bf16[1024,2048]{1,0:T(8,128)(2,1)}), bf16[128,2048]{1,0:T(8,128)(2,1)}) %reduce-scatter.45.cloned.1.call-update) | async-done | bytes 524304
  1034.6 9.8 convolution_add_fusion
  1062.9 81.8 %reduce-scatter.57.cloned.1.call-done = f32[32,3]{1,0:T(8,128)} async-done(((f32[1024,3]{1,0:T(8,128)}), f32[32,3]{1,0:T(8,128)}) %reduce-scatter.57.cloned.1.call-update) | async-done | bytes 400
  1146.0 131.5 %reduce-scatter.59.cloned.1.call-done = f32[32,3]{1,0:T(8,128)} async-done(((f32[1024,3]{1,0:T(8,128)}), f32[32,3]{1,0:T(8,128)}) %reduce-scatter.59.cloned.1.call-update) | async-done | bytes 400
  1288.9 129.8 %reduce-scatter.35.cloned.1.call-done = f32[32,1024]{1,0:T(8,128)} async-done(((f32[1024,1024]{1,0:T(8,128)}), f32[32,1024]{1,0:T(8,128)}) %reduce-scatter.35.cloned.1.call-update) | async-done | bytes 131088 | tf_op jit(solution)/shard_map/reduce_scatter | solution.py:354
  1418.8 142.8 %reduce-scatter.37.cloned.1.call-done = f32[32,1024]{1,0:T(8,128)} async-done(((f32[1024,1024]{1,0:T(8,128)}), f32[32,1024]{1,0:T(8,128)}) %reduce-scatter.37.cloned.1.call-update) | async-done | bytes 131088 | tf_op jit(solution)/shard_map/reduce_scatter | solution.py:357
  1561.6 142.8 %reduce-scatter.33.cloned.1.call-done = f32[32,1024]{1,0:T(8,128)} async-done(((f32[1024,1024]{1,0:T(8,128)}), f32[32,1024]{1,0:T(8,128)}) %reduce-scatter.33.cloned.1.call-update) | async-done | bytes 131088 | tf_op jit(solution)/shard_map/reduce_scatter | solution.py:353
  1704.4 142.0 %reduce-scatter.47.cloned.1.call-done = f32[32,1024]{1,0:T(8,128)} async-done(((f32[1024,1024]{1,0:T(8,128)}), f32[32,1024]{1,0:T(8,128)}) %reduce-scatter.47.cloned.1.call-update) | async-done | bytes 131088
  1846.4 142.4 %reduce-scatter.55.cloned.1.call-done = f32[32,1024]{1,0:T(8,128)} async-done(((f32[1024,1024]{1,0:T(8,128)}), f32[32,1024]{1,0:T(8,128)}) %reduce-scatter.55.cloned.1.call-update) | async-done | bytes 131088
  1988.8 142.6 %reduce-scatter.53.cloned.1.call-done = f32[32,1024]{1,0:T(8,128)} async-done(((f32[1024,1024]{1,0:T(8,128)}), f32[32,1024]{1,0:T(8,128)}) %reduce-scatter.53.cloned.1.call-update) | async-done | bytes 131088
  2131.4 142.1 %reduce-scatter.51.cloned.1.call-done = f32[32,1024]{1,0:T(8,128)} async-done(((f32[1024,1024]{1,0:T(8,128)}), f32[32,1024]{1,0:T(8,128)}) %reduce-scatter.51.cloned.1.call-update) | async-done | bytes 131088
  2273.5 142.7 %reduce-scatter.49.cloned.1.call-done = f32[32,1024]{1,0:T(8,128)} async-done(((f32[1024,1024]{1,0:T(8,128)}), f32[32,1024]{1,0:T(8,128)}) %reduce-scatter.49.cloned.1.call-update) | async-done | bytes 131088
  2416.2 185.8 %reduce-scatter.41.cloned.1.call-done = f32[128,1024]{1,0:T(8,128)} async-done(((f32[4096,1024]{1,0:T(8,128)}), f32[128,1024]{1,0:T(8,128)}) %reduce-scatter.41.cloned.1.call-update) | async-done | bytes 524304 | tf_op jit(solution)/shard_map/reduce_scatter | solution.py:359
  2602.0 187.3 %reduce-scatter.39.cloned.1.call-done = f32[32,4096]{1,0:T(8,128)} async-done(((f32[1024,4096]{1,0:T(8,128)}), f32[32,4096]{1,0:T(8,128)}) %reduce-scatter.39.cloned.1.call-update) | async-done | bytes 524304 | tf_op jit(solution)/shard_map/reduce_scatter | solution.py:358
  (548 shorter events, 320.8 us)
Async XLA Ops:
  7.2 63.0 %all-gather.21.cloned.1.call-start = ((), (), s32[]{:S(2)}) async-start(), calls=%async_computation.14 | async-start | bytes 2162688 | tf_op jit(solution)/shard_map/all_gather | solution.py:321
  7.9 120.6 %all-gather.25.cloned.1.call-start = ((), (), s32[]{:S(2)}) async-start(), calls=%async_computation.16 | async-start | bytes 2162688 | tf_op jit(solution)/shard_map/all_gather | solution.py:320
  8.7 239.2 %all-gather.29.cloned.1.call-start = ((), (), s32[]{:S(2)}) async-start(), calls=%async_computation.18 | async-start | bytes 2162688 | tf_op jit(solution)/shard_map/all_gather | solution.py:325
  9.4 241.3 %all-gather.33.cloned.1.call-start = ((), (), s32[]{:S(2)}) async-start(), calls=%async_computation.20 | async-start | bytes 2162688 | tf_op jit(solution)/shard_map/all_gather | solution.py:324
  10.0 293.9 %all-gather.23.cloned.1.call-start = ((), (), s32[]{:S(2)}) async-start(), calls=%async_computation.15 | async-start | bytes 2162688 | tf_op jit(solution)/shard_map/all_gather | solution.py:319
  10.6 323.3 %all-gather.41.cloned.1.call-start = ((), (), s32[]{:S(2)}) async-start(), calls=%async_computation.29 | async-start | bytes 2359296 | tf_op jit(solution)/shard_map/all_gather | solution.py:130
  73.1 291.6 %all-gather.43.cloned.1.call-start = ((), (), s32[]{:S(2)}) async-start(), calls=%async_computation.30 | async-start | bytes 2359296 | tf_op jit(solution)/shard_map/all_gather | solution.py:129
  131.3 292.3 %all-gather.27.cloned.1.call-start = ((), (), s32[]{:S(2)}) async-start(), calls=%async_computation.17 | async-start | bytes 2162688 | tf_op jit(solution)/shard_map/all_gather | solution.py:322
  132.1 349.9 %all-gather.31.cloned.1.call-start = ((), (), s32[]{:S(2)}) async-start(), calls=%async_computation.19 | async-start | bytes 2162688 | tf_op jit(solution)/shard_map/all_gather | solution.py:323
  132.8 379.2 %all-gather.45.cloned.1.call-start = ((), (), s32[]{:S(2)}) async-start(), calls=%async_computation.31 | async-start | bytes 2359296 | tf_op jit(solution)/shard_map/all_gather | solution.py:130
  134.1 408.2 %all-gather.47.cloned.1.call-start = ((), (), s32[]{:S(2)}) async-start(), calls=%async_computation.32 | async-start | bytes 2359296 | tf_op jit(solution)/shard_map/all_gather | solution.py:129
  136.9 464.2 %all-gather.35.cloned.1.call-start = ((), (), s32[]{:S(2)}) async-start(), calls=%async_computation.21 | async-start | bytes 2162688 | tf_op jit(solution)/shard_map/all_gather | solution.py:326
  137.5 542.8 %all-gather.37.cloned.1.call-start = ((), (), s32[]{:S(2)}) async-start(), calls=%async_computation.22 | async-start | bytes 8650752 | tf_op jit(solution)/shard_map/all_gather | solution.py:327
  138.2 620.9 %all-gather.39.cloned.1.call-start = ((), (), s32[]{:S(2)}) async-start(), calls=%async_computation.23 | async-start | bytes 8650752 | tf_op jit(solution)/shard_map/all_gather | solution.py:328
  138.8 782.5 %all-reduce.7.cloned.1.call-start = ((), (), s32[]{:S(2)}) async-start(), calls=%async_computation.42 | async-start | bytes 4194304
  246.2 523.8 %copy-start.86 = (f32[1,1024]{1,0:T(1,128)}, f32[1,1024]{1,0:T(1,128)S(1)}, u32[]{:S(2)}) copy-start(f32[1,1024]{1,0:T(1,128)S(1)} %get-tuple-element.154) | copy-start | bytes 12292
  254.6 349.0 %copy-start.79 = (bf16[128,1024]{0,1:T(8,128)(2,1)}, bf16[128,1024]{0,1:T(8,128)(2,1)S(1)}, u32[]{:S(2)}) copy-start(bf16[128,1024]{0,1:T(8,128)(2,1)S(1)} %copy.227) | copy-start | bytes 786436
  306.2 238.9 %copy-start.71 = (bf16[128,1024]{0,1:T(8,128)(2,1)}, bf16[128,1024]{0,1:T(8,128)(2,1)S(1)}, u32[]{:S(2)}) copy-start(bf16[128,1024]{0,1:T(8,128)(2,1)S(1)} %copy.223) | copy-start | bytes 786436
  844.3 115.9 %reduce-scatter.43.cloned.1.call-start = ((), (), s32[]{:S(2)}) async-start(), calls=%async_computation.33 | async-start | bytes 4718592
  857.2 153.3 %reduce-scatter.45.cloned.1.call-start = ((), (), s32[]{:S(2)}) async-start(), calls=%async_computation.34 | async-start | bytes 4718592
  881.3 263.3 %reduce-scatter.57.cloned.1.call-start = ((), (), s32[]{:S(2)}) async-start(), calls=%async_computation.40 | async-start | bytes 540672
  886.3 391.2 %reduce-scatter.59.cloned.1.call-start = ((), (), s32[]{:S(2)}) async-start(), calls=%async_computation.41 | async-start | bytes 540672
  887.5 531.3 %reduce-scatter.35.cloned.1.call-start = ((), (), s32[]{:S(2)}) async-start(), calls=%async_computation.25 | async-start | bytes 4325376 | tf_op jit(solution)/shard_map/reduce_scatter | solution.py:354
  892.6 669.0 %reduce-scatter.37.cloned.1.call-start = ((), (), s32[]{:S(2)}) async-start(), calls=%async_computation.26 | async-start | bytes 4325376 | tf_op jit(solution)/shard_map/reduce_scatter | solution.py:357
  897.4 807.0 %reduce-scatter.33.cloned.1.call-start = ((), (), s32[]{:S(2)}) async-start(), calls=%async_computation.24 | async-start | bytes 4325376 | tf_op jit(solution)/shard_map/reduce_scatter | solution.py:353
  902.0 944.4 %reduce-scatter.47.cloned.1.call-start = ((), (), s32[]{:S(2)}) async-start(), calls=%async_computation.35 | async-start | bytes 4325376
  919.5 1069.3 %reduce-scatter.55.cloned.1.call-start = ((), (), s32[]{:S(2)}) async-start(), calls=%async_computation.39 | async-start | bytes 4325376
  932.1 1199.3 %reduce-scatter.53.cloned.1.call-start = ((), (), s32[]{:S(2)}) async-start(), calls=%async_computation.38 | async-start | bytes 4325376
  942.9 1330.6 %reduce-scatter.51.cloned.1.call-start = ((), (), s32[]{:S(2)}) async-start(), calls=%async_computation.37 | async-start | bytes 4325376
  1020.7 1395.5 %reduce-scatter.49.cloned.1.call-start = ((), (), s32[]{:S(2)}) async-start(), calls=%async_computation.36 | async-start | bytes 4325376
  1029.6 1572.5 %reduce-scatter.41.cloned.1.call-start = ((), (), s32[]{:S(2)}) async-start(), calls=%async_computation.28 | async-start | bytes 17301504 | tf_op jit(solution)/shard_map/reduce_scatter | solution.py:359
  1044.5 1744.8 %reduce-scatter.39.cloned.1.call-start = ((), (), s32[]{:S(2)}) async-start(), calls=%async_computation.27 | async-start | bytes 17301504 | tf_op jit(solution)/shard_map/reduce_scatter | solution.py:358
  (143 other events, 2662.4 us)
Sparse Core Ops, SparseCore 0:
  11.0 59.1 all-gather.20
  73.2 55.3 all-gather.24
  131.6 55.3 all-gather.28
  189.8 55.3 all-gather.32
  248.0 55.8 all-gather.22
  305.9 27.9 all-gather.40
  336.1 28.5 all-gather.42
  367.7 55.9 all-gather.26
  426.7 55.3 all-gather.30
  484.0 27.9 all-gather.44
  513.6 28.5 all-gather.46
  545.1 55.9 all-gather.34
  604.1 76.1 all-gather.36
  683.1 75.9 all-gather.38
  844.4 63.6 all-reduce.6
  910.3 49.8 reduce-scatter.42
  962.3 48.1 reduce-scatter.44
  1012.6 131.9 reduce-scatter.56
  1147.0 130.5 reduce-scatter.58
  1280.2 138.4 reduce-scatter.34
  1421.6 139.9 reduce-scatter.36
  1564.4 139.8 reduce-scatter.32
  1707.2 139.1 reduce-scatter.46
  1849.1 139.6 reduce-scatter.54
  1991.6 139.7 reduce-scatter.52
  2134.1 139.3 reduce-scatter.50
  2276.2 139.9 reduce-scatter.48
  2419.1 182.9 reduce-scatter.40
  2604.9 184.3 reduce-scatter.38
where the time goes:
time: 2800 us
  waiting for transfers between devices  2340 us (84%)
  matrix products  192 us (7%)
  local copies, waits for them, and re-layouts  108 us (4%)
  blocking collectives  105 us (4%)
  other arithmetic  31.5 us (1%)
    unnamed x39, waiting for transfers between devices  998 us
    reduce_scatter x1, waiting for transfers between devices, shards(): lax.psum_scatter(totals[8], ('dp', 'seq'), scatter_dimension=0, tiled=True)  187 us
    reduce_scatter x1, waiting for transfers between devices, shards(): lax.psum_scatter(totals[9], ('dp', 'seq'), scatter_dimension=0, tiled=True)  186 us
    reduce_scatter x1, waiting for transfers between devices, shards(): lax.psum_scatter(totals[7], ('dp', 'seq'), scatter_dimension=0, tiled=True)  143 us
    reduce_scatter x1, waiting for transfers between devices, shards(): lax.psum_scatter(totals[3], ('dp', 'seq'), scatter_dimension=0, tiled=True)  143 us
    reduce_scatter x1, waiting for transfers between devices, shards(): lax.psum_scatter(totals[4], ('dp', 'seq'), scatter_dimension=0, tiled=True)  130 us
    unnamed x310, local copies, waits for them, and re-layouts  73.6 us
    all_gather x1, waiting for transfers between devices, shards(): lax.all_gather(expand_weight, ('dp', 'seq'), axis=0, tiled=True)  73.1 us
  transfers between devices with their start and end apart: 29, of which 26 were waited for; matrix products, arithmetic and copies ran while one was open for 8% of the time, Pallas kernels for 0%

commit v1 on v0

--- a/solution.py
+++ b/solution.py
@@ -1,11 +1,25 @@
+import functools
+
 import jax
 import jax.numpy as jnp
 from jax import lax
+from jax.experimental import pallas as pl
+from jax.experimental.pallas import tpu as pltpu
 from jax.sharding import PartitionSpec as P
 
 H = 16
 HD = 64
 MB = 2
+
+MESH = pl.DeviceIdType.MESH
+BF = jnp.bfloat16
+F32 = jnp.float32
+ALL = slice(None)
+D = 1024
+UNITS = 16
+SQUARE = 12
+GRID = (2, 2, 4, 2)
+VMEM_BYTES = 60 << 20
 
 
 alpha_scale = 300.0**0.25
@@ -379,9 +393,348 @@
     )
 
 
+class Place:
+    def __init__(self):
+        dp, seq = lax.axis_index("dp"), lax.axis_index("seq")
+        self.x, self.y, self.core, self.z = dp % 2, dp // 2, seq % 2, seq // 2
+
+    def at(self, y=None, x=None, z=None, core=None):
+        y = self.y if y is None else y
+        x = self.x if x is None else x
+        z = self.z if z is None else z
+        core = self.core if core is None else core
+        return (y * 2 + x, z * 2 + core)
+
+    def across(self, axis):
+        if axis == "x":
+            return self.at(x=1 - self.x)
+        if axis == "y":
+            return self.at(y=1 - self.y)
+        return self.at(core=1 - self.core)
+
+    def along_z(self, step):
+        return self.at(z=(self.z + step) % 4)
+
+    def greet(self):
+        barrier = pltpu.get_barrier_semaphore()
+        peers = [self.across(axis) for axis in ("x", "y", "core")]
+        peers += [self.along_z(step) for step in (1, 2, 3)]
+        for peer in peers:
+            pl.semaphore_signal(barrier, inc=1, device_id=peer, device_id_type=MESH)
+        pl.semaphore_wait(barrier, len(peers))
+
+
+def all_sum(place, part, total, work, send_sem, recv_sem):
+    def copy(number, send_slot, recv_slot, device):
+        return pltpu.make_async_remote_copy(
+            src_ref=work.at[0],
+            dst_ref=work.at[recv_slot],
+            send_sem=send_sem.at[send_slot],
+            recv_sem=recv_sem.at[recv_slot],
+            device_id=device,
+            device_id_type=MESH,
+        )
+
+    work[0] = part
+    for number, axis in enumerate(("core", "y", "x")):
+        step = copy(number, number, 1 + number, place.across(axis))
+        step.start()
+        step.wait()
+        work[0] = work[0] + work[1 + number]
+    steps = [copy(3, 2 + k, 4 + place.z, place.along_z(k)) for k in (1, 2, 3)]
+    for step in steps:
+        step.start()
+    result = work[0]
+    for k in (1, 2, 3):
+        source = (place.z + k) % 4
+        copy(3, 0, 4 + source, place.along_z(k)).wait_recv()
+        result = result + work[4 + source]
+    for step in steps:
+        step.wait_send()
+    total[...] = result
+
+
+def gather_kernel(own, norms, square, shrink, norms_all, work, send_sem, recv_sem, own_sem, sum_send, sum_recv):
+    place = Place()
+    y, x, z, core = place.y, place.x, place.z, place.core
+    place.greet()
+    sent = []
+
+    def block(unit, *index):
+        if unit < SQUARE:
+            return square.at[(unit,) + index]
+        return shrink.at[index + (unit - SQUARE,)]
+
+    def copy(unit, send_slot, recv_slot, source, target, device):
+        return pltpu.make_async_remote_copy(
+            src_ref=source,
+            dst_ref=target,
+            send_sem=send_sem.at[unit, send_slot],
+            recv_sem=recv_sem.at[unit, recv_slot],
+            device_id=device,
+            device_id_type=MESH,
+        )
+
+    def send(unit, send_slot, recv_slot, source, target, device):
+        step = copy(unit, send_slot, recv_slot, source, target, device)
+        step.start()
+        sent.append(step)
+
+    def share(unit, slot, part, device):
+        send(unit, slot, slot, part, part, device)
+
+    def arrived(unit, slot, target):
+        copy(unit, 0, slot, target, target, place.across("core")).wait_recv()
+
+    def phase(unit, number):
+        by_x = unit % 2 == 0
+        first, second = ("x", "y") if by_x else ("y", "x")
+        line = (y, x, ALL)
+        line_in = (y, 1 - x, ALL) if by_x else (1 - y, x, ALL)
+        sheet = (y, ALL, ALL) if by_x else (ALL, x, ALL)
+        sheet_in = (1 - y, ALL, ALL) if by_x else (ALL, 1 - x, ALL)
+        if number == 0:
+            for k in (1, 2, 3):
+                send(unit, k, z, own.at[unit], block(unit, y, x, z, core), place.along_z(k))
+        if number == 1:
+            pltpu.make_async_copy(own.at[unit], block(unit, y, x, z, core), own_sem.at[unit]).wait()
+            for k in (1, 2, 3):
+                source = (z + k) % 4
+                arrived(unit, source, block(unit, y, x, source, core))
+            share(unit, 4, block(unit, *line, core), place.across(first))
+            share(unit, 6, block(unit, *line, core), place.across("core"))
+        if number == 2:
+            arrived(unit, 4, block(unit, *line_in, core))
+            share(unit, 5, block(unit, *sheet, core), place.across(second))
+            share(unit, 7, block(unit, *line_in, core), place.across("core"))
+        if number == 3:
+            arrived(unit, 5, block(unit, *sheet_in, core))
+            share(unit, 8, block(unit, *sheet_in, core), place.across("core"))
+        if number == 4:
+            arrived(unit, 6, block(unit, *line, 1 - core))
+            arrived(unit, 7, block(unit, *line_in, 1 - core))
+            arrived(unit, 8, block(unit, *sheet_in, 1 - core))
+
+    for unit in range(UNITS):
+        pltpu.make_async_copy(own.at[unit], block(unit, y, x, z, core), own_sem.at[unit]).start()
+    for unit in range(4):
+        phase(unit, 0)
+    all_sum(place, norms[...], norms_all, work, sum_send, sum_recv)
+    pairs = UNITS // 2
+    for tick in range(1, pairs + 4):
+        for number in (0, 4, 3, 2, 1):
+            pair = tick + 1 if number == 0 else tick - number
+            if (2 if number == 0 else 0) <= pair < pairs:
+                for unit in (2 * pair, 2 * pair + 1):
+                    phase(unit, number)
+    for step in sent:
+        step.wait_send()
+
+
+def scatter_kernel(
+    square, shrink, norms, out, norms_all, held, from_core, from_first, from_second, from_z, work,
+    load_sem, send_sem, recv_sem, sum_send, sum_recv,
+):
+    place = Place()
+    y, x, z, core = place.y, place.x, place.z, place.core
+    place.greet()
+    slots = held.shape[0]
+    sent = {}
+
+    def load(unit):
+        source = square.at[unit] if unit < SQUARE else shrink.at[:, :, :, :, unit - SQUARE]
+        return pltpu.make_async_copy(source, held.at[unit % slots], load_sem.at[unit % slots])
+
+    def copy(unit, half, send_slot, recv_slot, source, target, device):
+        return pltpu.make_async_remote_copy(
+            src_ref=source,
+            dst_ref=target,
+            send_sem=send_sem.at[unit, half, send_slot],
+            recv_sem=recv_sem.at[unit, half, recv_slot],
+            device_id=device,
+            device_id_type=MESH,
+        )
+
+    def send(unit, half, send_slot, recv_slot, source, target, device):
+        step = copy(unit, half, send_slot, recv_slot, source, target, device)
+        step.start()
+        sent.setdefault(unit, []).append(step)
+
+    def arrived(unit, half, slot, target):
+        copy(unit, half, 0, slot, target, target, place.across("core")).wait_recv()
+
+    def add(total, part, count):
+        def one(index, _):
+            mine = total.at[index // 4] if count > 1 else total
+            theirs = part.at[index // 4] if count > 1 else part
+            row = index % 4
+            mine[row] = (mine[row].astype(F32) + theirs[row].astype(F32)).astype(BF)
+            return 0
+
+        lax.fori_loop(0, 4 * count, one, 0)
+
+    def phase(unit, half, number):
+        here = held.at[unit % slots]
+        rows = pl.ds(16 * half, 16)
+        by_y = half == 0
+        first, second = ("y", "x") if by_y else ("x", "y")
+        away = (1 - y, ALL) if by_y else (ALL, 1 - x)
+        keep = (y, ALL) if by_y else (ALL, x)
+        corner = (y, 1 - x) if by_y else (1 - y, x)
+        if number == 0:
+            send(unit, half, 0, 0, here.at[:, :, :, 1 - core, rows], from_core.at[unit, :, :, :, rows], place.across("core"))
+        if number == 1:
+            arrived(unit, half, 0, from_core.at[unit, :, :, :, rows])
+            add(here.at[(*away, ALL, core, rows)], from_core.at[(unit, *away, ALL, rows)], 2)
+            send(unit, half, 1, 1, here.at[(*away, ALL, core, rows)], from_first.at[unit, :, :, rows], place.across(first))
+            add(here.at[(*keep, ALL, core, rows)], from_core.at[(unit, *keep, ALL, rows)], 2)
+        if number == 2:
+            arrived(unit, half, 1, from_first.at[unit, :, :, rows])
+            other, mine = (1 - x, x) if by_y else (1 - y, y)
+            add(here.at[(*corner, ALL, core, rows)], from_first.at[unit, other, :, rows], 1)
+            send(unit, half, 2, 2, here.at[(*corner, ALL, core, rows)], from_second.at[unit, :, rows], place.across(second))
+            add(here.at[y, x, :, core, rows], from_first.at[unit, mine, :, rows], 1)
+        if number == 3:
+            arrived(unit, half, 2, from_second.at[unit, :, rows])
+            add(here.at[y, x, :, core, rows], from_second.at[unit, :, rows], 1)
+            for k in (1, 2, 3):
+                target = (z + k) % 4
+                send(unit, half, 3 + k, 4 + z, here.at[y, x, target, core, rows], from_z.at[unit, z, rows], place.along_z(k))
+        if number == 4:
+            total = here[y, x, z, core, rows].astype(F32)
+            for k in (1, 2, 3):
+                source = (z + k) % 4
+                arrived(unit, half, 4 + source, from_z.at[unit, source, rows])
+                total = total + from_z[unit, source, rows].astype(F32)
+            out[unit, rows] = total
+
+    for tick in range(UNITS + 4):
+        if tick < UNITS:
+            for unit in (0, 1, 2) if tick == 0 else (tick + 2,):
+                if unit < UNITS:
+                    for step in sent.pop(unit - slots, ()):
+                        step.wait_send()
+                    load(unit).start()
+            load(tick).wait()
+        for number in range(5):
+            unit = tick - number
+            if 0 <= unit < UNITS:
+                for half in (0, 1):
+                    phase(unit, half, number)
+        if tick == 3:
+            all_sum(place, norms[...], norms_all, work, sum_send, sum_recv)
+    for steps in sent.values():
+        for step in steps:
+            step.wait_send()
+
+
+IN_VMEM = pl.BlockSpec(memory_space=pltpu.VMEM)
+IN_PLACE = pl.BlockSpec(memory_space=pl.ANY)
+SQUARE_SHAPE = (SQUARE, *GRID, 32, D)
+SHRINK_SHAPE = (*GRID, UNITS - SQUARE, 32, D)
+
+
+def gather_weights(own, norms):
+    return pl.pallas_call(
+        gather_kernel,
+        in_specs=[IN_PLACE, IN_VMEM],
+        out_specs=(IN_PLACE, IN_PLACE, IN_VMEM),
+        out_shape=(
+            jax.ShapeDtypeStruct(SQUARE_SHAPE, BF),
+            jax.ShapeDtypeStruct(SHRINK_SHAPE, BF),
+            jax.ShapeDtypeStruct((8, D), F32),
+        ),
+        scratch_shapes=[
+            pltpu.VMEM((8, 8, D), F32),
+            pltpu.SemaphoreType.DMA((UNITS, 9)),
+            pltpu.SemaphoreType.DMA((UNITS, 9)),
+            pltpu.SemaphoreType.DMA((UNITS,)),
+            pltpu.SemaphoreType.DMA((8,)),
+            pltpu.SemaphoreType.DMA((8,)),
+        ],
+        compiler_params=pltpu.CompilerParams(
+            collective_id=0, has_side_effects=True, vmem_limit_bytes=VMEM_BYTES
+        ),
+    )(own, norms)
+
+
+def scatter_gradients(square, shrink, norms):
+    return pl.pallas_call(
+        scatter_kernel,
+        in_specs=[IN_PLACE, IN_PLACE, IN_VMEM],
+        out_specs=(IN_VMEM, IN_VMEM),
+        out_shape=(
+            jax.ShapeDtypeStruct((UNITS, 32, D), F32),
+            jax.ShapeDtypeStruct((8, D), F32),
+        ),
+        scratch_shapes=[
+            pltpu.VMEM((7, *GRID, 32, D), BF),
+            pltpu.VMEM((UNITS, 2, 2, 4, 32, D), BF),
+            pltpu.VMEM((UNITS, 2, 4, 32, D), BF),
+            pltpu.VMEM((UNITS, 4, 32, D), BF),
+            pltpu.VMEM((UNITS, 4, 32, D), BF),
+            pltpu.VMEM((8, 8, D), F32),
+            pltpu.SemaphoreType.DMA((7,)),
+            pltpu.SemaphoreType.DMA((UNITS, 2, 8)),
+            pltpu.SemaphoreType.DMA((UNITS, 2, 8)),
+            pltpu.SemaphoreType.DMA((8,)),
+            pltpu.SemaphoreType.DMA((8,)),
+        ],
+        compiler_params=pltpu.CompilerParams(
+            collective_id=1, has_side_effects=True, vmem_limit_bytes=VMEM_BYTES
+        ),
+    )(square, shrink, norms)
+
+
+def fast_shards(
+    tokens, memory, lengths, memory_segments, out_grad,
+    self_query, self_key, self_value, self_out,
+    cross_query, cross_key, cross_value, cross_out,
+    expand_weight, shrink_weight, norm_gains, norm_biases,
+):
+    me = lax.axis_index("dp") * lax.axis_size("seq") + lax.axis_index("seq")
+    squares = [self_query, self_key, self_value, self_out, cross_query, cross_key, cross_value, cross_out]
+    squares += [expand_weight[:, D * part : D * (part + 1)] for part in range(4)]
+    own = jnp.concatenate([jnp.stack(squares), shrink_weight.reshape(4, 32, D)])
+    norms = jnp.concatenate([norm_gains, norm_biases, jnp.zeros((2, 32), BF)]).astype(F32)
+    norms = lax.dynamic_update_slice(jnp.zeros((8, D), F32), norms, (0, 32 * me))
+    square, shrink, norms = gather_weights(own, norms)
+    square = square.reshape(SQUARE, D, D)
+    gathered = (
+        *(square[unit] for unit in range(8)),
+        square[8:].transpose(1, 0, 2).reshape(D, 4 * D),
+        shrink.reshape(4 * D, D),
+        norms[:3],
+        norms[3:6],
+    )
+    result, input_grad, memory_grad, gradients = micro_batch(
+        gathered, tokens, memory, lengths, memory_segments, out_grad
+    )
+    gradients = list(gradients)
+    expand_parts = [gradients[8][:, D * part : D * (part + 1)] for part in range(4)]
+    square_grads = jnp.stack([value.astype(BF) for value in gradients[:8] + expand_parts])
+    shrink_grads = gradients[9].astype(BF)
+    norm_grads = jnp.concatenate([gradients[10], gradients[11], jnp.zeros((2, D), F32)])
+    out, norm_grads = scatter_gradients(
+        square_grads.reshape(SQUARE_SHAPE), shrink_grads.reshape(SHRINK_SHAPE), norm_grads
+    )
+    norm_grads = lax.dynamic_slice(norm_grads, (0, 32 * me), (8, 32))
+    return (
+        result,
+        input_grad,
+        memory_grad,
+        *(out[unit] for unit in range(8)),
+        out[8:12].transpose(1, 0, 2).reshape(32, 4 * D),
+        out[12:].reshape(128, D),
+        norm_grads[:3],
+        norm_grads[3:6],
+    )
+
+
 def solution(mesh):
+    quick = dict(mesh.shape) == {"dp": 4, "seq": 8}
     return jax.shard_map(
-        shards,
+        fast_shards if quick else shards,
         mesh=mesh,
         in_specs=(
             P("dp", "seq", None),

time: 2800 us -> 786 us (0.28)
  waiting for transfers between devices: 2340 us -> 99.8 us
  Pallas kernels: 0 us -> 342 us
  blocking collectives: 105 us -> 17.2 us
  matrix products: 192 us -> 140 us
    unnamed x39 -> x5, waiting for transfers between devices: 998 us -> 0.08 us
    reduce_scatter x5 -> x3, waiting for transfers between devices: 789 us -> 67.3 us  [the longest x1 67.2 us: micro_batch(): lax.psum_scatter(jnp.concatenate([key_part.reshape(count, group_size, fea...]
    all_gather x10 -> x0, waiting for transfers between devices: 449 us -> none  [the longest x1 73.1 us: shards(): lax.all_gather(expand_weight, ('dp', 'seq'), axis=0, tiled=True)]
    pallas_call x0 -> x2, Pallas kernels: none -> 342 us  [the longest x1 176 us: gather_weights(): pl.pallas_call(gather_kernel, in_specs=[IN_PLACE, IN_VMEM], out_specs=(IN...]
    all_gather x2 -> x0, blocking collectives: 76.2 us -> none  [the longest x1 39.4 us: shards(): lax.all_gather(norm_gains, ('dp', 'seq'), axis=1, tiled=True)]
    all_gather x2 -> x1, waiting for transfers between devices: 52.7 us -> 1.28 us  [micro_batch(): lax.all_gather(own_keys, 'seq', axis=1, tiled=True)]
    slice x3 -> x8, local copies, waits for them, and re-layouts: 0.02 us -> 38.4 us  [the longest x2 19.9 us: fast_shards(): square[8:].transpose(1, 0, 2).reshape(D, 4 * D)]
    unnamed x310 -> x165, local copies, waits for them, and re-layouts: 73.6 us -> 37.3 us
  transfers between devices with their start and end apart: 29 -> 5, of which waited for: 26 -> 3; matrix products, arithmetic and copies ran while one was open for 8% -> 17% of each run, Pallas kernels for 0% -> 0%
where the time goes in v1:
time: 786 us; the launch traced here: 778 us
  Pallas kernels  342 us (44%)
  matrix products  140 us (18%)
  local copies, waits for them, and re-layouts  130 us (17%)
  waiting for transfers between devices  99.8 us (13%)
  other arithmetic  33.4 us (4%)
  blocking collectives  17.2 us (2%)
  between operations  15.2 us (2%)
    pallas_call x1, Pallas kernels, gather_weights(): pl.pallas_call(gather_kernel, in_specs=[IN_PLACE, IN_VMEM], out_specs=(IN...  176 us
    pallas_call x1, Pallas kernels, scatter_gradients(): pl.pallas_call(scatter_kernel, in_specs=[IN_PLACE, IN_PLACE, IN_VMEM], ou...  166 us
    reduce_scatter x1, waiting for transfers between devices, micro_batch(): lax.psum_scatter(jnp.concatenate([key_part.reshape(count, group_size, fea...  67.2 us
    unnamed x165, local copies, waits for them, and re-layouts  37.3 us
    all_gather x1, waiting for transfers between devices, micro_batch(): lax.all_gather(own_values, 'seq', axis=1, tiled=True)  31.2 us
    dot_general x10, matrix products, project_back(): lax.dot_general(left, right, (((1,), (1,)), ((), ())), preferred_element_...  28.7 us
    dot_general x10, matrix products, weight_term(): lax.dot_general(left, right, (((0,), (0,)), ((), ())), preferred_element_...  25 us
    dot_general x10, matrix products, project(): return jnp.dot(left, right, preferred_element_type=jnp.float32)  22.8 us
  transfers between devices with their start and end apart: 5, of which 3 were waited for; matrix products, arithmetic and copies ran while one was open for 17% of the time, Pallas kernels for 0%

profile of v1, /device:TPU:0, one launch (start us, length us, event | category | flops | bytes accessed | tf_op | source)
XLA Modules:
  0.0 777.7 jit_solution(5954731081433016632)
XLA Ops:
  20.1 175.7 %shard_map.280 = (bf16[12,2,2,4,2,32,1024]{6,5,4,3,2,1,0:T(8,128)(2,1)}, bf16[2,2,4,2,4,32,1024]{6,5,4,3,2,1,0:T(8,128)(2,1)}, f32[8,1024]{1,0:T(8,128)}) custom-call(bf16[16,32,1024]{2,1,0:T(8,128)(2,1)} %copy-done.56, f32[8,1024]{1,0:T(8,128)} %copy-done.63), custom_call_target="tpu_custom_call" | custom-call | tf_op jit(solution)/shard_map/pallas_call | solution.py:638
  195.8 11.3 %fusion.78 = (bf16[1,2,2,4,2,32,1024]{6,5,4,3,2,1,0:T(8,128)(2,1)}, bf16[1,2,2,4,2,32,1024]{6,5,4,3,2,1,0:T(8,128)(2,1)}, bf16[1,2,2,4,2,32,1024]{6,5,4,3,2,1,0:...) fusion(bf16[12,2,2,4,2,32,1024]{6,5,4,3,2,1,0:T(8,128)(2,1)} %g, ...), kind=kLoop, calls=%fused_computation.194 | loop fusion | bytes 33554432 | tf_op jit(solution)/shard_map/slice | solution.py:704
  210.0 3.1 convolution_convert_fusion.7
  213.2 8.5 %slice.156 = bf16[4,2,2,4,2,32,1024]{6,5,4,3,2,1,0:T(8,128)(2,1)} slice(bf16[12,2,2,4,2,32,1024]{6,5,4,3,2,1,0:T(8,128)(2,1)} %get-tuple-element.20), slice={[8:12], [0:2], [0:2], [0:4], [0:2], [0:32], [0:1024]} | slice | bytes 16777216 | tf_op jit(solution)/shard_map/slice | solution.py:705
  221.7 11.4 %copy.101 = bf16[4,1024,1024]{1,2,0:T(8,128)(2,1)} copy(bf16[4,1024,1024]{2,1,0:T(8,128)(2,1)} %bitcast.270) | data formatting | bytes 16777216 | tf_op jit(solution)/shard_map/slice | solution.py:705
  234.3 17.2 %all_gather.11 = bf16[2,128,1024]{2,1,0:T(8,128)(2,1)S(1)} all-gather(bf16[2,16,1024]{2,1,0:T(8,128)(2,1)S(1)} %copy-done.59), channel_id=1, replica_groups=mesh['dp'=4,'seq'=8] {'seq'}, dimensions={1}, use_global_device_ids=true | all-gather | bytes 589824 | tf_op jit(solution)/shard_map/all_gather | solution.py:159
  251.5 3.1 fusion.25
  262.3 6.2 copy.92
  268.5 5.0 fusion.84
  273.5 3.8 fusion
  279.2 31.2 %all-gather.3.cloned.1.call-done = bf16[2,1024,1024]{2,1,0:T(8,128)(2,1)} async-done(((bf16[2,128,1024]{2,1,0:T(8,128)(2,1)}), bf16[2,1024,1024]{2,1,0:T(8,128)(2,1)}) %all-gather.3.cloned.1.call-update) | async-done | bytes 4194320 | tf_op jit(solution)/shard_map/all_gather | solution.py:144
  310.4 6.2 copy.89
  316.6 9.2 %fusion.28 = bf16[2,128,16,64]{1,3,2,0:T(8,128)(2,1)S(1)} fusion(bf16[2,1024,16,64]{1,3,2,0:T(8,128)(2,1)} %bitcast.273, f32[2,16,128,1024]{3,2,1,0:T(8,128)} %copy-done, f32[2,16,128]{2,1,0:T(8,128)S(1)} %fusion, f32[2,16,128]{2,1,0:T(8,128)S(1)} %get-tuple-element.72), kind=kOutput, calls=%fused_computation.76 | convolution fusion | flops 549715968 | bytes 21528576 | tf_op jit(solution)/shard_map/ghqk,gkhd->gqhd/dot_general | solution.py:75
  339.3 7.8 %fusion.88 = (f32[256]{0:T(256)S(1)}, f32[256,1024]{1,0:T(8,128)S(1)}) fusion(bf16[4096,1024]{1,0:T(8,128)(2,1)} %bitcast.363, f32[256,4096]{1,0:T(8,128)S(1)} %fusion.71, f32[1024]{0:T(1024)S(1)} %bitcast.343, f32[1024]{0:T(1024)S(1)} %bitcast.337, f32[256]{0:T(256)S(1)} %fusion.65, f32[256,1024]{1,0:T(8,128)S(1)} %get-tuple-element.79, ...), kind=kOutput, calls=%fused_computation.204 | convolution fusion | flops 2158755584 | bytes 14691328 | tf_op jit(solution)/shard_map/dot_general | solution.py:38
  350.1 11.6 %fusion.12 = bf16[256,4096]{1,0:T(8,128)(2,1)S(1)} fusion(f32[256,4096]{1,0:T(8,128)} %copy-done.67, bf16[4096,1024]{1,0:T(8,128)(2,1)} %bitcast.364, f32[256,1024]{1,0:T(8,128)S(1)} %get-tuple-element.38, f32[256]{0:T(256)S(1)} %negate_multiply_fusion.2), kind=kOutput, calls=%fused_computation.23 | convolution fusion | flops 2168979456 | bytes 15729664 | tf_op jit(solution)/shard_map/dot_general | solution.py:42
  361.7 4.8 multiply_reduce_fusion.2
  371.9 2.8 copy.103
  385.8 2.8 copy.109
  388.6 16.8 %multiply_reduce_fusion = (f32[2,16,128]{2,1,0:T(8,128)S(1)}, f32[2,16,128,1024]{3,2,1,0:T(8,128)}) fusion(f32[2,16,128,1024]{3,2,1,0:T(8,128)} %copy-done, f32[2,16,128]{2,1,0:T(8,128)S(1)} %log_add_fusion, bf16[2,128,16,64]{1,3,2,0:T(8,128)(2,1)} %copy.109, bf16[2,1024,16,64]{1,3,2,0:T(8,128)(2,1)} %bitcast.274), kind=kOutput, calls=%fused_computation.1 | convolution fusion | flops 549449728 | bytes 38305792 | tf_op jit(solution)/shard_map/gqhd,gkhd->ghqk/dot_general | solution.py:84
  405.4 9.0 %fusion.13 = bf16[2,16,64,1024]{3,2,1,0:T(8,128)(2,1)} fusion(bf16[2,128,16,64]{1,3,2,0:T(8,128)(2,1)S(1)} %copy-done.30, f32[2,16,128,1024]{3,2,1,0:T(8,128)} %copy-done, f32[2,16,128]{2,1,0:T(8,128)S(1)} %log_add_fusion), kind=kOutput, calls=%fused_computation.29 | convolution fusion | flops 547356672 | bytes 21512192 | tf_op jit(solution)/shard_map/ghqk,gqhd->kghd/dot_general | solution.py:250
  417.7 6.3 copy.114
  426.1 15.3 %multiply_convert_fusion = bf16[2,16,128,1024]{3,2,1,0:T(8,128)(2,1)} fusion(f32[2,16,128,1024]{3,2,1,0:T(8,128)} %get-tuple-element.87, f32[2,16,128,1024]{3,2,1,0:T(8,128)} %copy-done, f32[2,16,128]{2,1,0:T(8,128)S(1)} %get-tuple-element.86, f32[2,16,128]{2,1,0:T(8,128)S(1)} %log_add_fusion), kind=kLoop, calls=%fused_computation | loop fusion | flops 16777216 | bytes 41975808 | tf_op jit(solution)/shard_map/convert_element_type | solution.py:88
  441.5 6.7 multiply_convert_fusion.1
  448.2 6.4 copy.113
  454.6 8.2 %pad_maximum_fusion = bf16[1024,2,2048]{2,0,1:T(8,128)(2,1)} fusion(bf16[1024,2,1024]{2,0,1:T(8,128)(2,1)} %copy.114, bf16[1024,2,1024]{2,0,1:T(8,128)(2,1)} %copy.113), kind=kLoop, calls=%fused_computation.9 | loop fusion | flops 16777216 | bytes 16777216 | tf_op jit(solution)/shard_map/concatenate | solution.py:254
  463.9 7.7 fusion.22
  487.8 4.3 fusion.79
  493.4 5.5 convolution_convert_fusion
  499.0 3.1 bitcast_convert_fusion.1
  502.1 3.0 bitcast_convert_fusion
  508.9 67.2 %reduce-scatter.4.cloned.1.call-done = bf16[128,2,2048]{2,0,1:T(8,128)(2,1)} async-done(((bf16[1024,2,2048]{2,0,1:T(8,128)(2,1)}), bf16[128,2,2048]{2,0,1:T(8,128)(2,1)}) %reduce-scatter.4.cloned.1.call-update) | async-done | bytes 1048592 | tf_op jit(solution)/shard_map/reduce_scatter | solution.py:253
  595.5 165.9 %shard_map.281 = (f32[16,32,1024]{2,1,0:T(8,128)}, f32[8,1024]{1,0:T(8,128)}) custom-call(bf16[12,2,2,4,2,32,1024]{6,5,4,3,2,1,0:T(8,128)(2,1)} %constant_dynamic-update-slice_fusion.1.square, bf16[2,2,4,2,4,32,1024]{6,5,4,3,2,1,0:T(8,128)(2,1)} %bitcast.275, f32[8,1024]{1,0:T(8,128)} %concatenate.17.norms), custom_call_target="tpu_custom_call" | custom-call | tf_op jit(solution)/shard_map/pallas_call | solution.py:662
  (268 shorter events, 115.5 us)
Async XLA Ops:
  7.2 255.1 %all-gather.5.cloned.1.call-start = ((), (), s32[]{:S(2)}) async-start(), calls=%async_computation.4 | async-start | bytes 4718592 | tf_op jit(solution)/shard_map/all_gather | solution.py:143
  195.8 12.7 %copy-start.22 = (bf16[2,128,1024]{2,1,0:T(8,128)(2,1)S(1)}, bf16[2,128,1024]{2,1,0:T(8,128)(2,1)}, u32[]{:S(2)}) copy-start(bf16[2,128,1024]{2,1,0:T(8,128)(2,1)} %param.17) | copy-start | bytes 1572868
  207.1 26.0 %copy-start.7 = (bf16[1,2,2,4,2,32,1024]{6,5,4,3,2,1,0:T(8,128)(2,1)}, bf16[1,2,2,4,2,32,1024]{6,5,4,3,2,1,0:T(8,128)(2,1)S(1)}, u32[]{:S(2)}) copy-start(bf16[1,2,2,4,2,32,1024]{6,5,4,3,2,1,0:T(8,128)(2,1)S(1)} %get-tuple-element.45) | copy-start | bytes 6291460
  210.0 100.4 %all-gather.3.cloned.1.call-start = ((), (), s32[]{:S(2)}) async-start(), calls=%async_computation.3 | async-start | bytes 4718592 | tf_op jit(solution)/shard_map/all_gather | solution.py:144
  213.2 285.8 %reduce-scatter.6.cloned.1.call-start = ((), (), s32[]{:S(2)}) async-start(), calls=%async_computation.6 | async-start | bytes 589824 | tf_op jit(solution)/shard_map/reduce_scatter | solution.py:219
  233.9 22.8 %copy-start.14 = (bf16[1,2,2,4,2,32,1024]{6,5,4,3,2,1,0:T(8,128)(2,1)S(1)}, bf16[1,2,2,4,2,32,1024]{6,5,4,3,2,1,0:T(8,128)(2,1)}, u32[]{:S(2)}) copy-start(bf16[1,2,2,4,2,32,1024]{6,5,4,3,2,1,0:T(8,128)(2,1)} %get-tuple-element.39) | copy-start | bytes 6291460
  234.0 34.4 %copy-start.31 = (bf16[2,128,16,64]{1,0,3,2:T(2,128)(2,1)}, bf16[2,128,16,64]{1,0,3,2:T(2,128)(2,1)S(1)}, u32[]{:S(2)}) copy-start(bf16[2,128,16,64]{1,0,3,2:T(2,128)(2,1)S(1)} %reshape_reshape.18) | copy-start | bytes 1572868
  254.7 5.7 copy-start.65
  254.7 5.8 copy-start.64
  273.5 5.7 copy-start
  316.6 9.8 %copy-start.9 = (bf16[1,2,2,4,2,32,1024]{6,5,4,3,2,1,0:T(8,128)(2,1)S(1)}, bf16[1,2,2,4,2,32,1024]{6,5,4,3,2,1,0:T(8,128)(2,1)}, u32[]{:S(2)}) copy-start(bf16[1,2,2,4,2,32,1024]{6,5,4,3,2,1,0:T(8,128)(2,1)} %get-tuple-element.43) | copy-start | bytes 6291460
  316.6 9.8 %copy-start.23 = (bf16[2,128,1024]{2,1,0:T(8,128)(2,1)S(1)}, bf16[2,128,1024]{2,1,0:T(8,128)(2,1)}, u32[]{:S(2)}) copy-start(bf16[2,128,1024]{2,1,0:T(8,128)(2,1)} %param.17) | copy-start | bytes 1572868
  336.0 30.5 %copy-start.1 = (f32[256,1024]{1,0:T(8,128)}, f32[256,1024]{1,0:T(8,128)S(1)}, u32[]{:S(2)}) copy-start(f32[256,1024]{1,0:T(8,128)S(1)} %get-tuple-element.79) | copy-start | bytes 3145732
  339.3 7.8 %copy-start.67 = (f32[256,4096]{1,0:T(8,128)}, f32[256,4096]{1,0:T(8,128)S(1)}, u32[]{:S(2)}) copy-start(f32[256,4096]{1,0:T(8,128)S(1)} %fusion.71) | copy-start | bytes 12582916
  339.3 8.1 %copy-start.39 = (bf16[2,128,1024]{2,1,0:T(8,128)(2,1)S(1)}, bf16[2,128,1024]{2,1,0:T(8,128)(2,1)}, u32[]{:S(2)}) copy-start(bf16[2,128,1024]{2,1,0:T(8,128)(2,1)} %param.21) | copy-start | bytes 1572868
  388.6 16.8 %copy-start.30 = (bf16[2,128,16,64]{1,3,2,0:T(8,128)(2,1)S(1)}, bf16[2,128,16,64]{1,3,2,0:T(8,128)(2,1)}, u32[]{:S(2)}) copy-start(bf16[2,128,16,64]{1,3,2,0:T(8,128)(2,1)} %copy.109) | copy-start | bytes 1572868
  405.4 9.0 %copy-start.6 = (bf16[2,16,128,128]{2,3,1,0:T(8,128)(2,1)S(1)}, bf16[2,16,128,128]{2,3,1,0:T(8,128)(2,1)}, u32[]{:S(2)}) copy-start(bf16[2,16,128,128]{2,3,1,0:T(8,128)(2,1)} %copy-done.5) | copy-start | bytes 3145732
  405.4 9.0 %copy-start.33 = (bf16[2,128,16,64]{1,3,2,0:T(8,128)(2,1)S(1)}, bf16[2,128,16,64]{1,3,2,0:T(8,128)(2,1)}, u32[]{:S(2)}) copy-start(bf16[2,128,16,64]{1,3,2,0:T(8,128)(2,1)} %copy.96) | copy-start | bytes 1572868
  405.4 10.6 %copy-start.34 = (bf16[2,128,16,64]{1,3,2,0:T(8,128)(2,1)S(1)}, bf16[2,128,16,64]{1,3,2,0:T(8,128)(2,1)}, u32[]{:S(2)}) copy-start(bf16[2,128,16,64]{1,3,2,0:T(8,128)(2,1)} %copy.103) | copy-start | bytes 1572868
  417.7 6.3 copy-start.55
  417.7 7.4 copy-start.54
  425.0 77.1 %reduce-scatter.8.cloned.1.call-start = ((), (), s32[]{:S(2)}) async-start(), calls=%async_computation.7 | async-start | bytes 589824 | tf_op jit(solution)/shard_map/reduce_scatter | solution.py:222
  426.1 15.4 %copy-start.32 = (bf16[2,128,16,64]{1,0,3,2:T(2,128)(2,1)S(1)}, bf16[2,128,16,64]{1,0,3,2:T(2,128)(2,1)}, u32[]{:S(2)}) copy-start(bf16[2,128,16,64]{1,0,3,2:T(2,128)(2,1)} %copy-done.31) | copy-start | bytes 1572868
  441.5 134.7 %reduce-scatter.4.cloned.1.call-start = ((), (), s32[]{:S(2)}) async-start(), calls=%async_computation.5 | async-start | bytes 9437184 | tf_op jit(solution)/shard_map/reduce_scatter | solution.py:253
  463.9 9.8 %copy-start.24 = (bf16[2,128,1024]{2,1,0:T(8,128)(2,1)S(1)}, bf16[2,128,1024]{2,1,0:T(8,128)(2,1)}, u32[]{:S(2)}) copy-start(bf16[2,128,1024]{2,1,0:T(8,128)(2,1)} %param.17) | copy-start | bytes 1572868
  487.8 5.7 copy-start.68
  493.4 5.6 copy-start.60
  499.0 8.5 %copy-start.15 = (bf16[1,2,2,4,2,32,1024]{6,5,4,3,2,1,0:T(8,128)(2,1)S(1)}, bf16[1,2,2,4,2,32,1024]{6,5,4,3,2,1,0:T(8,128)(2,1)}, u32[]{:S(2)}) copy-start(bf16[1,2,2,4,2,32,1024]{6,5,4,3,2,1,0:T(8,128)(2,1)} %get-tuple-element.39) | copy-start | bytes 6291460
  499.0 77.1 %copy-start.25 = (bf16[2,128,1024]{2,1,0:T(8,128)(2,1)S(1)}, bf16[2,128,1024]{2,1,0:T(8,128)(2,1)}, u32[]{:S(2)}) copy-start(bf16[2,128,1024]{2,1,0:T(8,128)(2,1)} %param.17) | copy-start | bytes 1572868
  499.0 6.1 copy-start.61
  761.4 6.8 copy-start.13
  761.4 6.8 copy-start.46
  (44 other events, 127.2 us)
Sparse Core Ops, SparseCore 0:
  210.1 52.1 all-gather.4
  264.4 45.9 all-gather.2
  425.1 29.6 reduce-scatter.5
  457.0 29.1 reduce-scatter.7
  488.4 87.6 reduce-scatter.3

commit v2 on v0

--- a/solution.py
+++ b/solution.py
@@ -1,6 +1,8 @@
 import jax
 import jax.numpy as jnp
 from jax import lax
+from jax.experimental import pallas as pl
+from jax.experimental.pallas import tpu as pltpu
 from jax.sharding import PartitionSpec as P
 
 H = 16
@@ -379,9 +381,1158 @@
     )
 
 
+MESH = pl.DeviceIdType.MESH
+BF = jnp.bfloat16
+F32 = jnp.float32
+ALL = slice(None)
+D = 1024
+LEN = 128
+OWN = 2 * LEN
+SPAN = 8 * LEN
+MEM = 128
+KEY, VALUE, QUERY, OUT, CROSS_QUERY, CROSS_KEY, CROSS_VALUE, CROSS_OUT = range(8)
+EXPAND = 8
+SQUARE = 12
+UNITS = 16
+GRID = (2, 2, 4, 2)
+SQUARE_SHAPE = (SQUARE, *GRID, 32, D)
+SHRINK_SHAPE = (*GRID, UNITS - SQUARE, 32, D)
+VMEM_BYTES = 60 << 20
+GELU_SLOPE = (2.0 / 3.141592653589793) ** 0.5
+GELU_CUBE = 0.044715
+
+
+class Place:
+    def __init__(self):
+        dp, seq = lax.axis_index("dp"), lax.axis_index("seq")
+        self.x, self.y, self.core, self.z, self.seq = dp % 2, dp // 2, seq % 2, seq // 2, seq
+        self.group = self.z // 2
+        self.low = seq % 4
+
+    def at(self, y=None, x=None, z=None, core=None):
+        y = self.y if y is None else y
+        x = self.x if x is None else x
+        z = self.z if z is None else z
+        core = self.core if core is None else core
+        return (y * 2 + x, z * 2 + core)
+
+    def across(self, axis):
+        if axis == "x":
+            return self.at(x=1 - self.x)
+        if axis == "y":
+            return self.at(y=1 - self.y)
+        return self.at(core=1 - self.core)
+
+    def along_z(self, step):
+        return self.at(z=(self.z + step) % 4)
+
+    def mate(self):
+        return self.at(z=self.z + 1 - 2 * (self.z % 2))
+
+    def greet(self):
+        barrier = pltpu.get_barrier_semaphore()
+        peers = [self.across(axis) for axis in ("x", "y", "core")]
+        peers += [self.along_z(step) for step in (1, 2, 3)]
+        for peer in peers:
+            pl.semaphore_signal(barrier, inc=1, device_id=peer, device_id_type=MESH)
+        pl.semaphore_wait(barrier, len(peers))
+
+
+class Links:
+    def __init__(self, place, send_sem, recv_sem):
+        self.place, self.send_sem, self.recv_sem = place, send_sem, recv_sem
+        self.sends, self.slots = 0, 0
+        self.open = {}
+
+    def slot(self, count=1):
+        first = self.slots
+        self.slots += count
+        assert self.slots <= self.recv_sem.shape[0]
+        return first
+
+    def send(self, slot, source, target, device):
+        assert self.sends < self.send_sem.shape[0]
+        step = pltpu.make_async_remote_copy(
+            src_ref=source,
+            dst_ref=target,
+            send_sem=self.send_sem.at[self.sends],
+            recv_sem=self.recv_sem.at[slot],
+            device_id=device,
+            device_id_type=MESH,
+        )
+        step.start()
+        self.sends += 1
+        self.open[id(step)] = step
+        return step
+
+    def arrived(self, slot, target):
+        pltpu.make_async_remote_copy(
+            src_ref=target,
+            dst_ref=target,
+            send_sem=self.send_sem.at[0],
+            recv_sem=self.recv_sem.at[slot],
+            device_id=self.place.across("core"),
+            device_id_type=MESH,
+        ).wait_recv()
+
+    def sent(self, step):
+        self.open.pop(id(step)).wait_send()
+
+    def finish(self):
+        for step in self.open.values():
+            step.wait_send()
+        self.open = {}
+
+
+class Moves:
+    def __init__(self, sem):
+        self.sem, self.count, self.open = sem, 0, {}
+
+    def start(self, source, target):
+        assert self.count < self.sem.shape[0]
+        step = pltpu.make_async_copy(source, target, self.sem.at[self.count])
+        step.start()
+        self.count += 1
+        self.open[id(step)] = step
+        return step
+
+    def wait(self, step):
+        self.open.pop(id(step)).wait()
+
+    def finish(self):
+        for step in self.open.values():
+            step.wait()
+        self.open = {}
+
+
+def all_sum(links, part, total, work):
+    place = links.place
+    work[0] = part[...]
+    for number, axis in enumerate(("core", "y", "x")):
+        slot = links.slot()
+        step = links.send(slot, work.at[0], work.at[1 + number], place.across(axis))
+        yield
+        links.arrived(slot, work.at[1 + number])
+        links.sent(step)
+        work[0] = work[0] + work[1 + number]
+    slot = links.slot(4)
+    for k in (1, 2, 3):
+        links.send(slot + place.z, work.at[0], work.at[4 + place.z], place.along_z(k))
+    yield
+    result = work[0]
+    for k in (1, 2, 3):
+        source = (place.z + k) % 4
+        links.arrived(slot + source, work.at[4 + source])
+        result = result + work[4 + source]
+    total[...] = result
+    yield
+
+
+def loop(count):
+    return pl.loop(0, count)
+
+
+def tile(index, size):
+    return pl.ds(pl.multiple_of(index * size, size), size)
+
+
+def rows_times(left, right, store, rows=OWN, width=256):
+    for first in range(0, left.shape[0], rows):
+
+        @loop(D // width)
+        def _(index):
+            columns = tile(index, width)
+            store(pl.ds(first, rows), columns, jnp.dot(left[pl.ds(first, rows), :], right[:, columns], preferred_element_type=F32))
+
+
+def rows_back(left, right, store, width=256):
+    @loop(D // width)
+    def _(index):
+        columns = tile(index, width)
+        store(columns, project_back(left[...], right[columns, :]))
+
+
+def put(target, dtype=BF):
+    def store(rows, columns, value):
+        target[rows, columns] = value.astype(dtype)
+
+    return store
+
+
+def half_masks():
+    lane = lax.broadcasted_iota(jnp.int32, (1, LEN), 1)
+    return [(lane < HD).astype(F32), (lane >= HD).astype(F32)]
+
+
+def attend_rows(queries, keys, values, bias, logs, out, segments):
+    masks = half_masks()
+    logs[...] = jnp.zeros_like(logs)
+
+    @loop(H // 2)
+    def _(pair):
+        columns = tile(pair, LEN)
+        for first, rows, count in segments:
+            own = pl.ds(first, rows)
+            key, value = keys[pl.ds(0, count), columns], values[pl.ds(0, count), columns]
+            query = queries[own, columns]
+            lane = lax.broadcasted_iota(jnp.int32, (rows, LEN), 1)
+            parts = []
+            for half in (0, 1):
+                scores = project_back(query * (masks[half] * HD**-0.5).astype(BF), key) + bias[own, pl.ds(0, count)]
+                top = jnp.max(scores, axis=1, keepdims=True)
+                powers = jnp.exp(scores - top)
+                total = jnp.sum(powers, axis=1, keepdims=True)
+                parts.append(project((powers * (1.0 / total)).astype(BF), value))
+                logs[own, :] = jnp.where(lane == 2 * pair + half, top + jnp.log(total), logs[own, :])
+            out[own, columns] = jnp.where(lane < HD, parts[0], parts[1]).astype(BF)
+
+
+def attend_rows_back(queries, keys, values, bias, logs, grads, query_grads, key_grads, value_grads, segments, pairs, first_pair=0):
+    masks = half_masks()
+
+    @loop(pairs)
+    def _(step):
+        pair = step + first_pair
+        columns = tile(pair, LEN)
+        for number, (first, rows, count) in enumerate(segments):
+            own, met = pl.ds(first, rows), pl.ds(0, count)
+            key, value = keys[met, columns], values[met, columns]
+            lane = lax.broadcasted_iota(jnp.int32, (rows, LEN), 1)
+            halves, score_lows, prob_lows, query_parts, grad_parts = [], [], [], [], []
+            for half in (0, 1):
+                query = queries[own, columns] * (masks[half] * HD**-0.5).astype(BF)
+                grad = grads[own, columns] * masks[half].astype(BF)
+                log_total = jnp.sum(jnp.where(lane == 2 * pair + half, logs[own, :], 0.0), axis=1, keepdims=True)
+                probs = jnp.exp(project_back(query, key) + bias[own, met] - log_total)
+                prob_grad = project_back(grad, value)
+                score_grad = probs * (prob_grad - jnp.sum(prob_grad * probs, axis=1, keepdims=True))
+                score_low = score_grad.astype(BF)
+                halves.append(project(score_low, key) * HD**-0.5)
+                score_lows.append(score_low)
+                prob_lows.append(probs.astype(BF))
+                query_parts.append(query)
+                grad_parts.append(grad)
+            query_grads[own, columns] = jnp.where(lane < HD, halves[0], halves[1]).astype(BF)
+            key_term = weight_term(jnp.concatenate(score_lows), jnp.concatenate(query_parts))
+            value_term = weight_term(jnp.concatenate(prob_lows), jnp.concatenate(grad_parts))
+            if number == 0:
+                key_grads[met, columns] = key_term.astype(BF)
+                value_grads[met, columns] = value_term.astype(BF)
+            else:
+                key_grads[met, columns] = (key_grads[met, columns].astype(F32) + key_term).astype(BF)
+                value_grads[met, columns] = (value_grads[met, columns].astype(F32) + value_term).astype(BF)
+
+
+SELF_SEGMENTS = ((LEN, LEN, SPAN), (0, LEN, SPAN // 2))
+CROSS_SEGMENTS = ((0, OWN, MEM),)
+STEP = 32
+
+
+def norm_rows(read, normal, inverse, emit):
+    @loop(OWN // STEP)
+    def _(index):
+        rows = tile(index, STEP)
+        value = read(rows)
+        centred = value - jnp.mean(value, axis=1, keepdims=True)
+        scale = lax.rsqrt(jnp.mean(centred * centred, axis=1, keepdims=True) + norm_eps)
+        result = centred * scale
+        if normal is not None:
+            normal[rows, :] = result
+            inverse[rows, :] = jnp.broadcast_to(scale, (STEP, LEN))
+        emit(rows, result, scale)
+
+
+def norm_rows_back(grad, normal, scale, gain, sums, number):
+    sums[pl.ds(number, 1), :] += jnp.sum(grad * normal, axis=0, keepdims=True)
+    sums[pl.ds(3 + number, 1), :] += jnp.sum(grad, axis=0, keepdims=True)
+    scaled = grad * gain
+    return scale * (
+        scaled
+        - jnp.mean(scaled, axis=1, keepdims=True)
+        - normal * jnp.mean(scaled * normal, axis=1, keepdims=True)
+    )
+
+
+class Gather:
+    ORDER = ((0, 1), (2, 3), (4, 5), (6, 7), (12, 13), (14, 15), (8, 9), (10, 11))
+
+    def __init__(self, links, moves, own, square, shrink):
+        self.links, self.moves, self.own, self.square, self.shrink = links, moves, own, square, shrink
+        self.slots = {unit: links.slot(9) for unit in range(UNITS)}
+        self.local = {unit: moves.start(own(unit), self.block(unit, *self.home())) for unit in range(UNITS)}
+        self.now = 0
+        self.sent_pairs = 0
+
+    def home(self):
+        place = self.links.place
+        return (place.y, place.x, place.z, place.core)
+
+    def block(self, unit, *index):
+        if unit < SQUARE:
+            return self.square.at[(unit,) + index]
+        return self.shrink.at[index + (unit - SQUARE,)]
+
+    def phase(self, unit, number):
+        links, place, slot = self.links, self.links.place, self.slots[unit]
+        y, x, z, core = self.home()
+        by_x = unit % 2 == 0
+        first, second = ("x", "y") if by_x else ("y", "x")
+        line = (y, x, ALL)
+        line_in = (y, 1 - x, ALL) if by_x else (1 - y, x, ALL)
+        sheet = (y, ALL, ALL) if by_x else (ALL, x, ALL)
+        sheet_in = (1 - y, ALL, ALL) if by_x else (ALL, 1 - x, ALL)
+
+        def share(number, index, device):
+            part = self.block(unit, *index, core)
+            links.send(slot + number, part, part, device)
+
+        def arrived(number, index, plane):
+            links.arrived(slot + number, self.block(unit, *index, plane))
+
+        if number == 0:
+            for k in (1, 2, 3):
+                links.send(slot + z, self.own(unit), self.block(unit, y, x, z, core), place.along_z(k))
+        if number == 1:
+            self.moves.wait(self.local[unit])
+            for k in (1, 2, 3):
+                arrived((z + k) % 4, (y, x, (z + k) % 4), core)
+            share(4, line, place.across(first))
+            share(6, line, place.across("core"))
+        if number == 2:
+            arrived(4, line_in, core)
+            share(5, sheet, place.across(second))
+            share(7, line_in, place.across("core"))
+        if number == 3:
+            arrived(5, sheet_in, core)
+            share(8, sheet_in, place.across("core"))
+        if number == 4:
+            arrived(6, line, 1 - core)
+            arrived(7, line_in, 1 - core)
+            arrived(8, sheet_in, 1 - core)
+
+    def tick(self):
+        if self.now == 0:
+            steps = [(0, 0), (1, 0)]
+        else:
+            steps = [(self.now + 1, 0)] + [(self.now - number, number) for number in (4, 3, 2, 1)]
+        for pair, number in steps:
+            if 0 <= pair < len(self.ORDER):
+                for unit in self.ORDER[pair]:
+                    self.phase(unit, number)
+        self.now += 1
+
+
+def core_rows(core, count=OWN):
+    return pl.ds(pl.multiple_of(core * count, count), count)
+
+
+def block_rows(block):
+    return pl.ds(pl.multiple_of(block * LEN, LEN), LEN)
+
+
+FORWARD_SAVES = {
+    "queries": ((OWN, D), BF),
+    "keys": ((SPAN, D), BF),
+    "values": ((SPAN, D), BF),
+    "self_bias": ((OWN, SPAN), F32),
+    "self_logs": ((OWN, LEN), F32),
+    "normal_one": ((OWN, D), F32),
+    "inverse_one": ((OWN, LEN), F32),
+    "cross_queries": ((OWN, D), BF),
+    "cross_keys": ((MEM, D), BF),
+    "cross_values": ((MEM, D), BF),
+    "cross_bias": ((OWN, MEM), F32),
+    "cross_logs": ((OWN, LEN), F32),
+    "normal_two": ((OWN, D), F32),
+    "inverse_two": ((OWN, LEN), F32),
+    "slopes": ((4, OWN, D), BF),
+    "third_grad": ((OWN, D), F32),
+    "norm_sums": ((8, D), F32),
+    "gains": ((8, D), F32),
+}
+TURNED_SAVES = {
+    "tokens_t": ((16, 32, 2 * OWN), BF),
+    "attended_t": ((16, 32, 2 * OWN), BF),
+    "first_t": ((16, 32, 2 * OWN), BF),
+    "cross_t": ((16, 32, 2 * OWN), BF),
+    "second_t": ((16, 32, 2 * OWN), BF),
+    "active_t": ((4, 4, 4, 32, 2 * OWN), BF),
+    "memory_t": ((16, 32, MEM), BF),
+    "branch": ((2 * OWN, D), BF),
+}
+FORWARD_SCRATCH = {
+    "stream": ((SPAN, D), BF),
+    "mine": ((OWN, D), BF),
+    "context": ((4, 2, 16, D), BF),
+    "attended": ((OWN, D), BF),
+    "first_low": ((OWN, D), BF),
+    "cross_attended": ((OWN, D), BF),
+    "second_low": ((OWN, D), BF),
+    "active": ((OWN, D), BF),
+    "sums": ((OWN, D), F32),
+    "final_low": ((OWN, D), BF),
+    "cotangent": ((OWN, D), BF),
+    "branch_own": ((OWN, D), BF),
+    "weights": ((4, D, D), BF),
+    "turned": ((3, 16, 2, 32, OWN), BF),
+    "turned_active": ((2, 4, 2, 4, 32, OWN), BF),
+    "turned_memory": ((16, 2, 32, MEM), BF),
+    "work": ((8, 8, D), F32),
+}
+FORWARD_SENDS, FORWARD_SLOTS, FORWARD_MOVES = 192, 224, 96
+
+
+class Refs:
+    def __init__(self, names, refs):
+        for name, ref in zip(names, refs):
+            setattr(self, name, ref)
+
+
+def forward_kernel(lengths, segments, norms, tokens, memory, out_grad, *refs):
+    squares, expand_own, shrink_own = refs[:8], refs[8], refs[9]
+    square, shrink, output = refs[10:13]
+    rest = refs[13:]
+    kept = Refs(FORWARD_SAVES, rest[: len(FORWARD_SAVES)])
+    rest = rest[len(FORWARD_SAVES) :]
+    turned = Refs(TURNED_SAVES, rest[: len(TURNED_SAVES)])
+    rest = rest[len(TURNED_SAVES) :]
+    held = Refs(FORWARD_SAVES, rest[: len(FORWARD_SAVES)])
+    rest = rest[len(FORWARD_SAVES) :]
+    held.__dict__.update(Refs(FORWARD_SCRATCH, rest[: len(FORWARD_SCRATCH)]).__dict__)
+    send_sem, recv_sem, move_sem = rest[len(FORWARD_SCRATCH) :]
+
+    place = Place()
+    links, moves = Links(place, send_sem, recv_sem), Moves(move_sem)
+    y, x, z, core, group, low, seq = place.y, place.x, place.z, place.core, place.group, place.low, place.seq
+    partner = place.across("core")
+    opposite = place.along_z(2)
+    mate = place.mate()
+    place.greet()
+
+    def own(unit):
+        if unit < EXPAND:
+            return squares[unit]
+        if unit < SQUARE:
+            return expand_own.at[:, pl.ds(D * (unit - EXPAND), D)]
+        return shrink_own.at[pl.ds(32 * (unit - SQUARE), 32)]
+
+    stream = held.stream
+    far, mate_seq = (seq + 4) % 8, (seq + 2) % 4 + 4 * group
+    other_seq = 2 * z + 1 - core
+    other_mate = (other_seq + 2) % 4 + 4 * group
+    slot_far, slot_mate, slot_mate_far, slot_core = links.slot(), links.slot(), links.slot(), links.slot(4)
+    home = moves.start(tokens.at[group], stream.at[block_rows(seq)])
+    links.send(slot_far, tokens.at[1 - group], stream.at[block_rows(seq)], opposite)
+    links.send(slot_mate, tokens.at[group], stream.at[block_rows(seq)], mate)
+    links.send(slot_core, tokens.at[group], stream.at[block_rows(seq)], partner)
+    gather = Gather(links, moves, own, square, shrink)
+    gather.tick()
+    slot_memory, slot_context = links.slot(4), links.slot()
+    context_home = moves.start(memory.at[group], held.context.at[z, core])
+    for k in (1, 2, 3):
+        links.send(slot_memory + z, memory.at[((z + k) % 4) // 2], held.context.at[z, core], place.along_z(k))
+    norm_steps = all_sum(links, norms, held.gains, held.work)
+    next(norm_steps)
+
+    def sentence(places):
+        result, end = jnp.zeros_like(places), 0
+        for index in range(lengths.shape[1] - 1):
+            end = end + lengths[group, index]
+            result = result + (places >= end).astype(jnp.int32)
+        return result
+
+    held.norm_sums[...] = jnp.zeros_like(held.norm_sums)
+
+    @loop(OWN // STEP)
+    def _(index):
+        row = index * STEP + lax.broadcasted_iota(jnp.int32, (STEP, 1), 0)
+        row_place = LEN * low + row + jnp.where(row >= LEN, 3 * LEN, 0)
+        row_sentence = sentence(row_place)
+        key_place = lax.broadcasted_iota(jnp.int32, (1, SPAN), 1)
+        allowed = (row_sentence == sentence(key_place)) & (key_place <= row_place)
+        held.self_bias[tile(index, STEP), :] = jnp.where(allowed, 0.0, masked_score)
+        met = row_sentence == segments[pl.ds(group, 1), :]
+        held.cross_bias[tile(index, STEP), :] = jnp.where(met, 0.0, masked_score)
+
+    def pass_on(number, block):
+        links.send(slot_core + number, stream.at[block_rows(block)], stream.at[block_rows(block)], partner)
+
+    links.arrived(slot_far, stream.at[block_rows(far)])
+    links.send(slot_mate_far, stream.at[block_rows(far)], stream.at[block_rows(far)], mate)
+    pass_on(1, far)
+    gather.tick()
+    next(norm_steps)
+    moves.wait(context_home)
+    for k in (1, 2, 3):
+        links.arrived(slot_memory + (z + k) % 4, held.context.at[(z + k) % 4, core])
+    links.send(slot_context, held.context.at[:, core], held.context.at[:, core], partner)
+    links.arrived(slot_mate, stream.at[block_rows(mate_seq)])
+    pass_on(2, mate_seq)
+    gather.tick()
+    next(norm_steps)
+    cotangent_rows, cotangent_far = block_rows(group), block_rows(1 - group)
+    slot_cotangent = links.slot()
+    cotangent_home = moves.start(out_grad.at[group], held.cotangent.at[cotangent_rows])
+    links.send(slot_cotangent, out_grad.at[1 - group], held.cotangent.at[cotangent_rows], opposite)
+    links.arrived(slot_mate_far, stream.at[block_rows((mate_seq + 4) % 8)])
+    pass_on(3, (mate_seq + 4) % 8)
+    moves.wait(home)
+    for number, block in enumerate((other_seq, (other_seq + 4) % 8, other_mate, (other_mate + 4) % 8)):
+        links.arrived(slot_core + number, stream.at[block_rows(block)])
+    links.arrived(slot_context, held.context.at[:, 1 - core])
+    gather.tick()
+    next(norm_steps)
+    held.mine[pl.ds(0, LEN), :] = stream[block_rows(low), :]
+    held.mine[pl.ds(LEN, LEN), :] = stream[block_rows(low + 4), :]
+
+    loads = {}
+
+    def fetch(unit, slot):
+        source = square.at[unit].reshape(D, D) if unit < SQUARE else shrink.at[(unit - SQUARE) // 2, unit % 2].reshape(D, D)
+        loads[unit] = (moves.start(source, held.weights.at[slot]), slot)
+
+    def weight(unit):
+        step, slot = loads.pop(unit)
+        moves.wait(step)
+        return held.weights.at[slot]
+
+    turning = {"count": 0, "open": {}}
+    landing = []
+    mine, theirs = core_rows(core), core_rows(1 - core)
+
+    def turn(source, name):
+        number = turning["count"] % 3
+        for move, sent in turning["open"].pop(number, ()):
+            moves.wait(move)
+            links.sent(sent)
+        turning["count"] += 1
+        buffer, target = held.turned.at[number], getattr(turned, name)
+
+        @loop(4)
+        def _(index):
+            buffer[pl.ds(4 * index, 4)] = source[:, tile(index, OWN)].T.reshape(4, 2, 32, OWN)
+
+        slot = links.slot()
+        move = moves.start(buffer.at[:, core], target.at[:, :, mine])
+        sent = links.send(slot, buffer.at[:, 1 - core], target.at[:, :, mine], partner)
+        landing.append((slot, target.at[:, :, theirs]))
+        turning["open"][number] = [(move, sent)]
+
+    def keep(*names):
+        for name in names:
+            moves.start(getattr(held, name), getattr(kept, name))
+
+    def gain(number):
+        return held.gains[pl.ds(number, 1), :]
+
+    def bias(number):
+        return held.gains[pl.ds(3 + number, 1), :]
+
+    gather.tick()
+    fetch(KEY, 0)
+    fetch(VALUE, 1)
+    turn(held.mine, "tokens_t")
+    next(norm_steps)
+    rows_times(stream, weight(KEY), put(held.keys))
+    gather.tick()
+    fetch(QUERY, 2)
+    fetch(OUT, 3)
+    rows_times(stream, weight(VALUE), put(held.values))
+    rows_times(held.mine, weight(QUERY), put(held.queries))
+    attend_rows(held.queries, held.keys, held.values, held.self_bias, held.self_logs, held.attended, SELF_SEGMENTS)
+    gather.tick()
+    fetch(CROSS_QUERY, 0)
+    fetch(CROSS_KEY, 1)
+    keep("queries", "keys", "values", "self_bias", "self_logs", "cross_bias", "gains")
+    rows_times(held.attended, weight(OUT), put(held.sums, F32))
+
+    def first_rows(rows, result, _):
+        held.first_low[rows, :] = (result * gain(0) + bias(0)).astype(BF)
+
+    def after(rows, previous):
+        return held.sums[rows, :] + alpha_scale * previous
+
+    norm_rows(lambda rows: after(rows, held.mine[rows, :].astype(F32)), held.normal_one, held.inverse_one, first_rows)
+    turn(held.attended, "attended_t")
+    rows_times(held.first_low, weight(CROSS_QUERY), put(held.cross_queries))
+    context = held.context.reshape(MEM, D)
+    rows_times(context, weight(CROSS_KEY), put(held.cross_keys), MEM)
+    gather.tick()
+    fetch(CROSS_VALUE, 2)
+    fetch(CROSS_OUT, 3)
+    turn(held.first_low, "first_t")
+
+    @loop(4)
+    def _(index):
+        held.turned_memory[pl.ds(4 * index, 4)] = context[:, tile(index, OWN)].T.reshape(4, 2, 32, MEM)
+
+    moves.start(held.turned_memory.at[:, core], turned.memory_t)
+    rows_times(context, weight(CROSS_VALUE), put(held.cross_values), MEM)
+    attend_rows(
+        held.cross_queries, held.cross_keys, held.cross_values, held.cross_bias, held.cross_logs,
+        held.cross_attended, CROSS_SEGMENTS,
+    )
+    keep("cross_queries", "cross_keys", "cross_values", "cross_logs", "normal_one", "inverse_one")
+    rows_times(held.cross_attended, weight(CROSS_OUT), put(held.sums, F32))
+
+    def second_rows(rows, result, _):
+        held.second_low[rows, :] = (result * gain(1) + bias(1)).astype(BF)
+
+    norm_rows(
+        lambda rows: after(rows, held.normal_one[rows, :] * gain(0) + bias(0)),
+        held.normal_two, held.inverse_two, second_rows,
+    )
+    keep("normal_two", "inverse_two")
+    gather.tick()
+    turn(held.cross_attended, "cross_t")
+    turn(held.second_low, "second_t")
+    gather.tick()
+    held.sums[...] = jnp.zeros_like(held.sums)
+    turned_open = {}
+    for part in range(4):
+        if part % 2 == 0:
+            gather.tick()
+            for number in (0, 1):
+                fetch(EXPAND + part + number, 2 * number)
+                fetch(SQUARE + part + number, 2 * number + 1)
+        expand = weight(EXPAND + part)
+        slopes = held.slopes.at[part]
+
+        def activate(rows, columns, value):
+            inner = GELU_SLOPE * (value + GELU_CUBE * value * value * value)
+            bend = jnp.tanh(inner)
+            held.active[rows, columns] = (0.5 * value * (1.0 + bend)).astype(BF)
+            slope = 0.5 * (1.0 + bend) + 0.5 * value * (1.0 - bend * bend) * (
+                GELU_SLOPE * (1.0 + 3.0 * GELU_CUBE * value * value)
+            )
+            slopes[rows, columns] = slope.astype(BF)
+
+        def add(rows, columns, value):
+            held.sums[rows, columns] += value
+
+        rows_times(held.second_low, expand, activate)
+        rows_times(held.active, weight(SQUARE + part), add)
+        number = part % 2
+        for move, sent in turned_open.pop(number, ()):
+            moves.wait(move)
+            links.sent(sent)
+        buffer = held.turned_active.at[number]
+
+        @loop(4)
+        def _(index):
+            buffer[index] = held.active[:, tile(index, OWN)].T.reshape(2, 4, 32, OWN)
+
+        slot = links.slot()
+        move = moves.start(buffer.at[:, core], turned.active_t.at[part, :, :, :, mine])
+        sent = links.send(slot, buffer.at[:, 1 - core], turned.active_t.at[part, :, :, :, mine], partner)
+        landing.append((slot, turned.active_t.at[part, :, :, :, theirs]))
+        turned_open[number] = [(move, sent)]
+    keep("slopes")
+    links.arrived(slot_cotangent, held.cotangent.at[cotangent_far])
+    moves.wait(cotangent_home)
+
+    def third_rows(rows, result, scale):
+        held.final_low[rows, :] = (result * gain(2) + bias(2)).astype(BF)
+        grad = norm_rows_back(held.cotangent[rows, :].astype(F32), result, scale, gain(2), held.norm_sums, 2)
+        held.third_grad[rows, :] = grad
+        held.branch_own[rows, :] = grad.astype(BF)
+
+    norm_rows(lambda rows: after(rows, held.normal_two[rows, :] * gain(1) + bias(1)), None, None, third_rows)
+    slot = links.slot()
+    links.send(slot, held.branch_own, turned.branch.at[mine], partner)
+    landing.append((slot, turned.branch.at[theirs]))
+    moves.start(held.branch_own, turned.branch.at[mine])
+    keep("third_grad", "norm_sums")
+    slot = links.slot()
+    moves.start(held.final_low.at[block_rows(group)], output.at[group])
+    links.send(slot, held.final_low.at[block_rows(1 - group)], output.at[group], opposite)
+    for arrival in landing:
+        links.arrived(*arrival)
+    links.arrived(slot, output.at[1 - group])
+    moves.finish()
+    links.finish()
+
+
+IN_VMEM = pl.BlockSpec(memory_space=pltpu.VMEM)
+IN_SMEM = pl.BlockSpec(memory_space=pltpu.SMEM)
+IN_PLACE = pl.BlockSpec(memory_space=pl.ANY)
+
+
+def shapes_of(table):
+    return [jax.ShapeDtypeStruct(shape, dtype) for shape, dtype in table.values()]
+
+
+def vmem_of(table):
+    return [pltpu.VMEM(shape, dtype) for shape, dtype in table.values()]
+
+
+def forward_call(lengths, segments, norms, tokens, memory, out_grad, weights):
+    results = [
+        jax.ShapeDtypeStruct(SQUARE_SHAPE, BF),
+        jax.ShapeDtypeStruct(SHRINK_SHAPE, BF),
+        jax.ShapeDtypeStruct(tokens.shape, BF),
+        *shapes_of(FORWARD_SAVES),
+        *shapes_of(TURNED_SAVES),
+    ]
+    values = pl.pallas_call(
+        forward_kernel,
+        in_specs=[IN_SMEM, IN_VMEM, IN_VMEM] + [IN_PLACE] * 13,
+        out_specs=[IN_PLACE] * len(results),
+        out_shape=results,
+        scratch_shapes=[
+            *vmem_of(FORWARD_SAVES),
+            *vmem_of(FORWARD_SCRATCH),
+            pltpu.SemaphoreType.DMA((FORWARD_SENDS,)),
+            pltpu.SemaphoreType.DMA((FORWARD_SLOTS,)),
+            pltpu.SemaphoreType.DMA((FORWARD_MOVES,)),
+        ],
+        compiler_params=pltpu.CompilerParams(collective_id=0, has_side_effects=True, vmem_limit_bytes=VMEM_BYTES),
+    )(lengths, segments, norms, tokens, memory, out_grad, *weights)
+    saves = dict(zip([*FORWARD_SAVES, *TURNED_SAVES], values[3:]))
+    return values[0], values[1], values[2], saves
+
+
+class Scatter:
+    def __init__(self, links, grads, from_first, from_second, from_z, result):
+        self.links, self.grads, self.result = links, grads, result
+        self.from_first, self.from_second, self.from_z = from_first, from_second, from_z
+        self.slots, self.pending, self.now = {}, {}, 0
+
+    def home(self, unit):
+        for step in self.pending.pop(unit - self.grads.shape[0], ()):
+            self.links.sent(step)
+        self.slots[unit] = self.links.slot(12)
+        return self.grads.at[unit % self.grads.shape[0]]
+
+    def add(self, total, part):
+        for row in range(4):
+            total[row] = (total[row].astype(F32) + part[row].astype(F32)).astype(BF)
+
+    def phase(self, unit, half, number):
+        links, place = self.links, self.links.place
+        y, x, z = place.y, place.x, place.z
+        here = self.grads.at[unit % self.grads.shape[0]]
+        depth = unit % self.from_first.shape[0]
+        rows = pl.ds(16 * half, 16)
+        slot = self.slots[unit] + 6 * half
+        by_y = half == 0
+        first, second = ("y", "x") if by_y else ("x", "y")
+        away = (1 - y, ALL) if by_y else (ALL, 1 - x)
+        corner, other, mine = ((y, 1 - x), 1 - x, x) if by_y else ((1 - y, x), 1 - y, y)
+        home = here.at[y, x, :, rows]
+        first_in = self.from_first.at[depth, :, :, rows]
+        second_in = self.from_second.at[depth, :, rows]
+
+        def send(number, source, target, device):
+            self.pending.setdefault(unit, []).append(links.send(slot + number, source, target, device))
+
+        if number == 0:
+            send(0, here.at[(*away, ALL, rows)], first_in, place.across(first))
+        if number == 1:
+            links.arrived(slot, first_in)
+            corner_part = here.at[(*corner, ALL, rows)]
+            self.add(corner_part, first_in.at[other])
+            send(1, corner_part, second_in, place.across(second))
+            self.add(home, first_in.at[mine])
+        if number == 2:
+            links.arrived(slot + 1, second_in)
+            self.add(home, second_in)
+            for k in (1, 2, 3):
+                send(2 + z, home.at[(z + k) % 4], self.from_z.at[depth, z, rows], place.along_z(k))
+        if number == 3:
+            total = home[z].astype(F32)
+            for k in (1, 2, 3):
+                source = (z + k) % 4
+                links.arrived(slot + 2 + source, self.from_z.at[depth, source, rows])
+                total = total + self.from_z[depth, source, rows].astype(F32)
+            self.result(unit, rows, total)
+
+    def tick(self):
+        for number in (3, 2, 1, 0):
+            unit = self.now - number
+            if 0 <= unit < UNITS:
+                for half in (0, 1):
+                    self.phase(unit, half, number)
+        self.now += 1
+
+
+DEPTH = 4
+BACKWARD_SCRATCH = {
+    "weights": ((3, D, D), BF),
+    "grads": ((6, 2, 2, 4, 32, D), BF),
+    "from_first": ((DEPTH, 2, 4, 32, D), BF),
+    "from_second": ((DEPTH, 4, 32, D), BF),
+    "from_z": ((DEPTH, 4, 32, D), BF),
+    "up": ((4, 2 * OWN, D), BF),
+    "second_sum": ((OWN, D), F32),
+    "cross_branch": ((2 * OWN, D), BF),
+    "attended_grad": ((OWN, D), BF),
+    "cross_query_grad": ((2 * OWN, D), BF),
+    "cross_terms": ((2, 2, MEM, D), BF),
+    "cross_sums": ((2, MEM, D), BF),
+    "self_branch": ((2 * OWN, D), BF),
+    "query_grad": ((2 * OWN, D), BF),
+    "terms": ((2, 2, 2, 2, LEN, D), BF),
+    "terms_core": ((2, 2, 2, LEN, D), BF),
+    "terms_mate": ((2, 2, LEN, D), BF),
+    "key_grad": ((2 * OWN, D), BF),
+    "value_grad": ((2 * OWN, D), BF),
+    "memory_own": ((4, 16, D), BF),
+    "memory_in": ((4, 16, D), BF),
+    "far_own": ((LEN, D), BF),
+    "far_in": ((LEN, D), BF),
+    "work": ((8, 8, D), F32),
+}
+BACKWARD_SENDS, BACKWARD_SLOTS, BACKWARD_MOVES = 240, 256, 64
+
+
+def backward_kernel(square, shrink, *refs):
+    names = [*FORWARD_SAVES, *TURNED_SAVES]
+    kept = Refs(names, refs[: len(names)])
+    rest = refs[len(names) :]
+    input_grad, memory_grad, unit_grads, expand_grad, shrink_grad, norm_grads = rest[0], rest[1], rest[2:10], *rest[10:13]
+    rest = rest[13:]
+    held = Refs(names, rest[: len(names)])
+    rest = rest[len(names) :]
+    held.__dict__.update(Refs(BACKWARD_SCRATCH, rest[: len(BACKWARD_SCRATCH)]).__dict__)
+    send_sem, recv_sem, move_sem = rest[len(BACKWARD_SCRATCH) :]
+
+    place = Place()
+    links, moves = Links(place, send_sem, recv_sem), Moves(move_sem)
+    z, core, group = place.z, place.core, place.group
+    partner = place.across("core")
+    mine, theirs = core_rows(core), core_rows(1 - core)
+    loads = {}
+
+    def bring(*wanted):
+        for name in wanted:
+            loads[name] = moves.start(getattr(kept, name), getattr(held, name))
+
+    def have(*wanted):
+        for name in wanted:
+            moves.wait(loads.pop(name))
+
+    def fetch(unit, slot):
+        source = square.at[unit].reshape(D, D) if unit < SQUARE else shrink.at[(unit - SQUARE) // 2, unit % 2].reshape(D, D)
+        loads[unit] = moves.start(source, held.weights.at[slot])
+
+    def weight(unit, slot):
+        moves.wait(loads.pop(unit))
+        return held.weights.at[slot]
+
+    bring("branch", "active_t")
+    fetch(SQUARE, 0)
+    fetch(EXPAND, 1)
+    fetch(SQUARE + 1, 2)
+    bring("slopes", "third_grad", "second_t", "norm_sums", "gains", "normal_two", "inverse_two")
+    bring("cross_queries", "cross_keys", "cross_values", "cross_bias", "cross_logs", "cross_t")
+    bring("normal_one", "inverse_one", "first_t", "memory_t", "attended_t", "tokens_t")
+    bring("queries", "keys", "values", "self_bias", "self_logs")
+    place.greet()
+
+    order = [12, 13, 14, 15, 8, 9, 10, 11, CROSS_OUT, CROSS_QUERY, CROSS_KEY, CROSS_VALUE, OUT, QUERY, KEY, VALUE]
+
+    def result(number, rows, total):
+        unit = order[number]
+        if unit < EXPAND:
+            unit_grads[unit][rows, :] = total
+        elif unit < SQUARE:
+            expand_grad[rows, pl.ds(D * (unit - EXPAND), D)] = total
+        else:
+            shrink_grad[pl.ds(32 * (unit - SQUARE) + rows.start, rows.size), :] = total
+
+    scatter = Scatter(links, held.grads, held.from_first, held.from_second, held.from_z, result)
+    made = {"count": 0}
+
+    def produce(left, right, depth=2 * OWN):
+        target = scatter.home(made["count"])
+        made["count"] += 1
+
+        @loop(4)
+        def _(index):
+            columns = tile(index, OWN)
+            term = project(left().reshape(512, depth), right[:, columns])
+            target[:, :, :, :, columns] = term.astype(BF).reshape(2, 2, 4, 32, OWN)
+
+    def share(ref):
+        slot = links.slot()
+        links.send(slot, ref.at[mine], ref.at[mine], partner)
+        return slot
+
+    def shared(ref, slot):
+        links.arrived(slot, ref.at[theirs])
+
+    def gain(number):
+        return held.gains[pl.ds(number, 1), :]
+
+    have("branch", "active_t")
+
+    def produce_shrink(part):
+        produce(lambda: held.active_t[:, :, part], held.branch)
+
+    def produce_expand(part):
+        shared(held.up.at[part], up_slots[part])
+        produce(lambda: held.second_t[...], held.up.at[part])
+
+    produce_shrink(0)
+    scatter.tick()
+    for part in (1, 2, 3):
+        produce_shrink(part)
+    scatter.tick()
+    have("slopes")
+    own_branch = held.branch.at[mine]
+    up_slots = []
+    for part in range(4):
+        if part == 2:
+            scatter.tick()
+        up = held.up.at[part, mine]
+        slopes = held.slopes.at[part]
+
+        def bend(columns, value):
+            up[:, columns] = (value * slopes[:, columns].astype(F32)).astype(BF)
+
+        rows_back(own_branch, weight(SQUARE + part, 2 * part % 3), bend)
+        up_slots.append(share(held.up.at[part]))
+        if part < 3:
+            fetch(EXPAND + part + 1, 2 * part % 3)
+
+        def add(columns, value):
+            if part == 0:
+                held.second_sum[:, columns] = value
+            else:
+                held.second_sum[:, columns] += value
+
+        rows_back(up, weight(EXPAND + part, (2 * part + 1) % 3), add)
+        fetch((SQUARE + 2, SQUARE + 3, CROSS_OUT, CROSS_QUERY)[part], (2 * part + 1) % 3)
+    fetch(CROSS_KEY, 0)
+    scatter.tick()
+    have("third_grad", "norm_sums", "gains", "normal_two", "inverse_two", "second_t")
+
+    def spread(inverse, rows):
+        return inverse[rows, pl.ds(0, 1)]
+
+    @loop(OWN // STEP)
+    def _(index):
+        rows = tile(index, STEP)
+        grad = held.second_sum[rows, :] + alpha_scale * held.third_grad[rows, :]
+        pre = norm_rows_back(grad, held.normal_two[rows, :], spread(held.inverse_two, rows), gain(1), held.norm_sums, 1)
+        held.second_sum[rows, :] = pre
+        held.cross_branch[pl.ds(pl.multiple_of(OWN * core + STEP * index, STEP), STEP), :] = pre.astype(BF)
+
+    slot_cross_branch = share(held.cross_branch)
+    produce_expand(0)
+    scatter.tick()
+
+    def low(target):
+        def store(columns, value):
+            target[:, columns] = value.astype(BF)
+
+        return store
+
+    rows_back(held.cross_branch.at[mine], weight(CROSS_OUT, 2), low(held.attended_grad))
+    fetch(CROSS_VALUE, 2)
+    have("cross_queries", "cross_keys", "cross_values", "cross_bias", "cross_logs", "cross_t")
+    attend_rows_back(
+        held.cross_queries, held.cross_keys, held.cross_values, held.cross_bias, held.cross_logs, held.attended_grad,
+        held.cross_query_grad.at[mine], held.cross_terms.at[0, core], held.cross_terms.at[1, core], CROSS_SEGMENTS, H // 2,
+    )
+    slot_cross_query = share(held.cross_query_grad)
+    slot_cross_terms = links.slot()
+    links.send(slot_cross_terms, held.cross_terms.at[:, core], held.cross_terms.at[:, core], partner)
+    produce_expand(1)
+    scatter.tick()
+
+    def add_first(columns, value):
+        held.third_grad[:, columns] = value
+
+    rows_back(held.cross_query_grad.at[mine], weight(CROSS_QUERY, 1), add_first)
+    fetch(OUT, 1)
+    have("normal_one", "inverse_one", "first_t", "memory_t", "attended_t", "tokens_t")
+
+    @loop(OWN // STEP)
+    def _(index):
+        rows = tile(index, STEP)
+        grad = held.third_grad[rows, :] + alpha_scale * held.second_sum[rows, :]
+        pre = norm_rows_back(grad, held.normal_one[rows, :], spread(held.inverse_one, rows), gain(0), held.norm_sums, 0)
+        held.second_sum[rows, :] = pre
+        held.self_branch[pl.ds(pl.multiple_of(OWN * core + STEP * index, STEP), STEP), :] = pre.astype(BF)
+
+    slot_self_branch = share(held.self_branch)
+    norm_steps = all_sum(links, held.norm_sums, norm_grads, held.work)
+    next(norm_steps)
+    produce_expand(2)
+    scatter.tick()
+    rows_back(held.self_branch.at[mine], weight(OUT, 1), low(held.attended_grad))
+    fetch(QUERY, 1)
+    have("queries", "keys", "values", "self_bias", "self_logs")
+    terms = held.terms
+
+    def attend_part(first, pairs):
+        attend_rows_back(
+            held.queries, held.keys, held.values, held.self_bias, held.self_logs, held.attended_grad,
+            held.query_grad.at[mine], terms.at[0].reshape(SPAN, D), terms.at[1].reshape(SPAN, D), SELF_SEGMENTS, pairs, first,
+        )
+
+    attend_part(0, 2)
+    produce_expand(3)
+    scatter.tick()
+    next(norm_steps)
+    attend_part(2, 2)
+    shared(held.cross_branch, slot_cross_branch)
+    produce(lambda: held.cross_t[...], held.cross_branch)
+    scatter.tick()
+    next(norm_steps)
+    attend_part(4, 2)
+    shared(held.cross_query_grad, slot_cross_query)
+    produce(lambda: held.first_t[...], held.cross_query_grad)
+    scatter.tick()
+    next(norm_steps)
+    attend_part(6, 2)
+    slot_query = share(held.query_grad)
+    slot_terms = links.slot()
+    links.send(slot_terms, terms.at[:, :, :, 1 - core], held.terms_core, partner)
+
+    links.arrived(slot_cross_terms, held.cross_terms.at[:, 1 - core])
+    for which in (0, 1):
+        held.cross_sums[which] = (held.cross_terms[which, 0].astype(F32) + held.cross_terms[which, 1].astype(F32)).astype(BF)
+    produce(lambda: held.memory_t[...], held.cross_sums.at[0], MEM)
+    scatter.tick()
+    next(norm_steps)
+
+    links.arrived(slot_terms, held.terms_core)
+    near = z % 2
+
+    def join(place_index):
+        for which in (0, 1):
+            for high in (0, 1):
+                value = terms[which, high, place_index, core].astype(F32) + held.terms_core[which, high, place_index].astype(F32)
+                terms[which, high, place_index, core] = value.astype(BF)
+
+    join(1 - near)
+    slot_mate = links.slot()
+    links.send(slot_mate, terms.at[:, :, 1 - near, core], held.terms_mate, place.mate())
+    join(near)
+
+    produce(lambda: held.memory_t[...], held.cross_sums.at[1], MEM)
+    scatter.tick()
+    key_rows = held.cross_sums[0].reshape(4, 2, 16, D)
+
+    cross_key, cross_value = weight(CROSS_KEY, 0), weight(CROSS_VALUE, 2)
+    sums = held.cross_sums.reshape(2, 4, 2, 16, D)
+
+    @loop(4)
+    def _(index):
+        columns = tile(index, OWN)
+        term = project_back(sums[0, :, core].reshape(64, D), cross_key[columns, :])
+        term = term + project_back(sums[1, :, core].reshape(64, D), cross_value[columns, :])
+        held.memory_own[:, :, columns] = term.astype(BF).reshape(4, 16, OWN)
+
+    fetch(KEY, 0)
+    fetch(VALUE, 2)
+    slot_memory = links.slot(4)
+    for k in (1, 2, 3):
+        links.send(slot_memory + z, held.memory_own.at[(z + k) % 4], held.memory_in.at[z], place.along_z(k))
+    held.memory_in[z] = held.memory_own[z]
+
+    shared(held.self_branch, slot_self_branch)
+    produce(lambda: held.attended_t[...], held.self_branch)
+    scatter.tick()
+    shared(held.query_grad, slot_query)
+    produce(lambda: held.tokens_t[...], held.query_grad)
+    scatter.tick()
+
+    def add_input(columns, value):
+        held.third_grad[:, columns] = alpha_scale * held.second_sum[:, columns] + value
+
+    rows_back(held.query_grad.at[mine], weight(QUERY, 1), add_input)
+    links.arrived(slot_mate, held.terms_mate)
+    for which, target in enumerate((held.key_grad, held.value_grad)):
+        for high in (0, 1):
+            value = terms[which, high, near, core].astype(F32) + held.terms_mate[which, high].astype(F32)
+            target[pl.ds(pl.multiple_of(OWN * core + LEN * high, LEN), LEN), :] = value.astype(BF)
+    slot_key, slot_value = share(held.key_grad), share(held.value_grad)
+    shared(held.key_grad, slot_key)
+    produce(lambda: held.tokens_t[...], held.key_grad)
+    scatter.tick()
+    shared(held.value_grad, slot_value)
+    produce(lambda: held.tokens_t[...], held.value_grad)
+    scatter.tick()
+
+    def add_more(columns, value):
+        held.third_grad[:, columns] += value
+
+    rows_back(held.key_grad.at[mine], weight(KEY, 0), add_more)
+    rows_back(held.value_grad.at[mine], weight(VALUE, 2), add_more)
+    held.far_own[...] = held.third_grad[block_rows(1 - group), :].astype(BF)
+    slot_far = links.slot()
+    links.send(slot_far, held.far_own, held.far_in, place.along_z(2))
+    input_grad[group] = held.third_grad[block_rows(group), :]
+    scatter.tick()
+    for k in (1, 2, 3):
+        links.arrived(slot_memory + (z + k) % 4, held.memory_in.at[(z + k) % 4])
+    for which in (0, 1):
+        memory_grad[which] = held.memory_in[2 * which].astype(F32) + held.memory_in[2 * which + 1].astype(F32)
+    links.arrived(slot_far, held.far_in)
+    input_grad[1 - group] = held.far_in[...].astype(F32)
+    scatter.tick()
+    scatter.tick()
+    moves.finish()
+    links.finish()
+
+
+def backward_call(square, shrink, saves, block_shape, memory_shape):
+    results = [jax.ShapeDtypeStruct(block_shape, F32), jax.ShapeDtypeStruct(memory_shape, F32)]
+    results += [jax.ShapeDtypeStruct((32, D), F32)] * 8
+    results += [jax.ShapeDtypeStruct(shape, F32) for shape in ((32, 4 * D), (LEN, D), (8, D))]
+    saved = {**FORWARD_SAVES, **TURNED_SAVES}
+    return pl.pallas_call(
+        backward_kernel,
+        in_specs=[IN_PLACE] * (2 + len(saved)),
+        out_specs=[IN_VMEM] * len(results),
+        out_shape=results,
+        scratch_shapes=[
+            *vmem_of(saved),
+            *vmem_of(BACKWARD_SCRATCH),
+            pltpu.SemaphoreType.DMA((BACKWARD_SENDS,)),
+            pltpu.SemaphoreType.DMA((BACKWARD_SLOTS,)),
+            pltpu.SemaphoreType.DMA((BACKWARD_MOVES,)),
+        ],
+        compiler_params=pltpu.CompilerParams(collective_id=1, has_side_effects=True, vmem_limit_bytes=63 << 20),
+    )(square, shrink, *(saves[name] for name in saved))
+
+
+def fast_shards(
+    tokens, memory, lengths, memory_segments, out_grad,
+    self_query, self_key, self_value, self_out,
+    cross_query, cross_key, cross_value, cross_out,
+    expand_weight, shrink_weight, norm_gains, norm_biases,
+):
+    me = lax.axis_index("dp") * lax.axis_size("seq") + lax.axis_index("seq")
+    norms = jnp.concatenate([norm_gains, norm_biases, jnp.zeros((2, 32), BF)]).astype(F32)
+    norms = lax.dynamic_update_slice(jnp.zeros((8, D), F32), norms, (0, 32 * me))
+    weights = (self_key, self_value, self_query, self_out, cross_query, cross_key, cross_value, cross_out)
+    square, shrink, output, saves = forward_call(
+        lengths, memory_segments, norms, tokens, memory, out_grad, (*weights, expand_weight, shrink_weight)
+    )
+    values = backward_call(square, shrink, saves, tokens.shape, memory.shape)
+    input_grad, memory_grad, units, expand_grad, shrink_grad, norm_grads = values[0], values[1], values[2:10], *values[10:]
+    norm_grads = lax.dynamic_slice(norm_grads, (0, 32 * me), (8, 32))
+    return (
+        output,
+        input_grad,
+        memory_grad,
+        *(units[unit] for unit in (QUERY, KEY, VALUE, OUT, CROSS_QUERY, CROSS_KEY, CROSS_VALUE, CROSS_OUT)),
+        expand_grad,
+        shrink_grad,
+        norm_grads[:3],
+        norm_grads[3:6],
+    )
+
+
 def solution(mesh):
+    quick = dict(mesh.shape) == {"dp": 4, "seq": 8}
     return jax.shard_map(
-        shards,
+        fast_shards if quick else shards,
         mesh=mesh,
         in_specs=(
             P("dp", "seq", None),

time: 2800 us -> 426 us (0.15)
  waiting for transfers between devices: 2340 us -> 0 us
  Pallas kernels: 0 us -> 411 us
  matrix products: 192 us -> 0 us
  blocking collectives: 105 us -> 0 us
  local copies, waits for them, and re-layouts: 108 us -> 13 us
  other arithmetic: 31.5 us -> 0.77 us
    unnamed x39 -> x0, waiting for transfers between devices: 998 us -> none
    reduce_scatter x5 -> x0, waiting for transfers between devices: 789 us -> none  [the longest x1 187 us: shards(): lax.psum_scatter(totals[8], ('dp', 'seq'), scatter_dimension=0, tiled=True)]
    all_gather x14 -> x0, waiting for transfers between devices: 554 us -> none  [the longest x1 73.1 us: shards(): lax.all_gather(expand_weight, ('dp', 'seq'), axis=0, tiled=True)]
    pallas_call x0 -> x2, Pallas kernels: none -> 411 us  [the longest x1 219 us: forward_call(): pl.pallas_call(forward_kernel, in_specs=[IN_SMEM, IN_VMEM, IN_VMEM] + [IN...]
    dot_general x84 -> x0, matrix products: 192 us -> none  [the longest x20 57.9 us: weight_term(): lax.dot_general(left, right, (((0,), (0,)), ((), ())), preferred_element_...]
    all_gather x4 -> x0, blocking collectives: 105 us -> none  [the longest x1 39.4 us: shards(): lax.all_gather(norm_gains, ('dp', 'seq'), axis=1, tiled=True)]
    unnamed x310 -> x39, local copies, waits for them, and re-layouts: 73.6 us -> 11.3 us
  transfers between devices with their start and end apart: 29 -> 0, of which waited for: 26 -> 0; matrix products, arithmetic and copies ran while one was open for 8% -> 0% of each run, Pallas kernels for 0% -> 0%
where the time goes in v2:
time: 426 us
  Pallas kernels  411 us (96%)
  local copies, waits for them, and re-layouts  13 us (3%)
    pallas_call x1, Pallas kernels, forward_call(): pl.pallas_call(forward_kernel, in_specs=[IN_SMEM, IN_VMEM, IN_VMEM] + [IN...  219 us
    pallas_call x1, Pallas kernels, backward_call(): pl.pallas_call(backward_kernel, in_specs=[IN_PLACE] * (2 + len(saved)), o...  192 us
    unnamed x39, local copies, waits for them, and re-layouts  11.3 us

profile of v2, /device:TPU:0, one launch (start us, length us, event | category | flops | bytes accessed | tf_op | source)
XLA Modules:
  0.0 425.6 jit_solution(7148267329648164019)
XLA Ops:
  0.7 0.1 pad.2.clone
  0.7 0.8 maximum_convert_fusion
  1.5 0.2 dynamic_update_slice.3.norms
  1.7 0.0 copy-start.3
  1.7 0.6 copy-done.3
  2.3 218.9 %shard_map.280 = (bf16[12,2,2,4,2,32,1024]{6,5,4,3,2,1,0:T(8,128)(2,1)}, bf16[2,2,4,2,4,32,1024]{6,5,4,3,2,1,0:T(8,128)(2,1)}, bf16[2,128,1024]{2,1,0:T(8,128)(2...) custom-call(s32[2,8]{1,0:T(2,128)} %lengths.1, ...), custom_call_target="tpu_custom_call" | custom-call | tf_op jit(solution)/shard_map/pallas_call | solution.py:1077
  221.2 0.0 copy-start.2
  221.2 192.2 %shard_map.281 = (f32[2,128,1024]{2,1,0:T(8,128)}, f32[2,16,1024]{2,1,0:T(8,128)}, f32[32,1024]{1,0:T(8,128)}, f32[32,1024]{1,0:T(8,128)}, f32[32,1024]{1,0:T(8,...) custom-call(bf16[12,2,2,4,2,32,1024]{6,5,4,3,2,1,0:T(8,128)(2,1)} %g, ...), custom_call_target="tpu_custom_call" | custom-call | tf_op jit(solution)/shard_map/pallas_call | solution.py:1488
  413.4 0.0 copy-start.12
  413.4 0.0 copy-start.11
  413.4 0.0 copy-start.10
  413.5 0.0 copy-start.9
  413.5 0.8 constant_dynamic-slice_fusion
  414.3 0.6 fusion
  414.9 0.0 copy-done.2
  414.9 0.8 copy.46
  415.7 2.4 copy.47
  418.1 0.0 copy-done.12
  418.1 0.7 copy.48
  418.7 0.0 copy-done.11
  418.7 0.7 copy.49
  419.4 0.0 copy-done.10
  419.4 0.7 copy.50
  420.1 0.0 copy-done.9
  420.1 0.7 copy.51
  420.7 0.7 copy.52
  421.4 0.7 copy.53
  422.0 0.7 copy.54
  422.7 0.7 copy.55
  423.4 0.7 copy.56
  424.0 0.8 copy.57
  424.8 0.8 copy.58
  (16 shorter events, 0.0 us)
Async XLA Ops:
  1.7 0.6 copy-start.3
  221.2 193.7 %copy-start.2 = (bf16[2,128,1024]{2,1,0:T(8,128)(2,1)S(1)}, bf16[2,128,1024]{2,1,0:T(8,128)(2,1)}, u32[]{:S(2)}) copy-start(bf16[2,128,1024]{2,1,0:T(8,128)(2,1)} %get-tuple-element.116) | copy-start | bytes 1572868
  413.4 4.7 %copy-start.12 = (f32[2,16,1024]{2,1,0:T(8,128)S(1)}, f32[2,16,1024]{2,1,0:T(8,128)}, u32[]{:S(2)}) copy-start(f32[2,16,1024]{2,1,0:T(8,128)} %get-tuple-element.118) | copy-start | bytes 393220
  413.4 5.3 %copy-start.11 = (f32[32,1024]{1,0:T(8,128)S(1)}, f32[32,1024]{1,0:T(8,128)}, u32[]{:S(2)}) copy-start(f32[32,1024]{1,0:T(8,128)} %get-tuple-element.119) | copy-start | bytes 393220
  413.4 6.0 %copy-start.10 = (f32[32,1024]{1,0:T(8,128)S(1)}, f32[32,1024]{1,0:T(8,128)}, u32[]{:S(2)}) copy-start(f32[32,1024]{1,0:T(8,128)} %get-tuple-element.120) | copy-start | bytes 393220
  413.5 6.6 %copy-start.9 = (f32[32,1024]{1,0:T(8,128)S(1)}, f32[32,1024]{1,0:T(8,128)}, u32[]{:S(2)}) copy-start(f32[32,1024]{1,0:T(8,128)} %get-tuple-element.121) | copy-start | bytes 393220
  414.9 5.8 %copy-start.8 = (f32[32,1024]{1,0:T(8,128)S(1)}, f32[32,1024]{1,0:T(8,128)}, u32[]{:S(2)}) copy-start(f32[32,1024]{1,0:T(8,128)} %get-tuple-element.122) | copy-start | bytes 393220
  414.9 6.5 %copy-start.7 = (f32[32,1024]{1,0:T(8,128)S(1)}, f32[32,1024]{1,0:T(8,128)}, u32[]{:S(2)}) copy-start(f32[32,1024]{1,0:T(8,128)} %get-tuple-element.123) | copy-start | bytes 393220
  415.7 6.4 %copy-start.6 = (f32[32,1024]{1,0:T(8,128)S(1)}, f32[32,1024]{1,0:T(8,128)}, u32[]{:S(2)}) copy-start(f32[32,1024]{1,0:T(8,128)} %get-tuple-element.124) | copy-start | bytes 393220
  415.7 7.0 %copy-start.5 = (f32[32,1024]{1,0:T(8,128)S(1)}, f32[32,1024]{1,0:T(8,128)}, u32[]{:S(2)}) copy-start(f32[32,1024]{1,0:T(8,128)} %get-tuple-element.125) | copy-start | bytes 393220
  415.7 7.7 %copy-start.4 = (f32[32,1024]{1,0:T(8,128)S(1)}, f32[32,1024]{1,0:T(8,128)}, u32[]{:S(2)}) copy-start(f32[32,1024]{1,0:T(8,128)} %get-tuple-element.126) | copy-start | bytes 393220
  415.7 8.3 %copy-start.1 = (f32[32,4096]{1,0:T(8,128)S(1)}, f32[32,4096]{1,0:T(8,128)}, u32[]{:S(2)}) copy-start(f32[32,4096]{1,0:T(8,128)} %get-tuple-element.127) | copy-start | bytes 1572868
  418.1 6.7 %copy-start = (f32[128,1024]{1,0:T(8,128)S(1)}, f32[128,1024]{1,0:T(8,128)}, u32[]{:S(2)}) copy-start(f32[128,1024]{1,0:T(8,128)} %get-tuple-element.128) | copy-start | bytes 1572868

commit v3 on v2

--- a/solution.py
+++ b/solution.py
@@ -564,12 +564,12 @@
     return [(lane < HD).astype(F32), (lane >= HD).astype(F32)]
 
 
-def attend_rows(queries, keys, values, bias, logs, out, segments):
+def attend_rows(queries, keys, values, bias, logs, out, segments, pairs=H // 2, first_pair=0):
     masks = half_masks()
-    logs[...] = jnp.zeros_like(logs)
-
-    @loop(H // 2)
-    def _(pair):
+
+    @loop(pairs)
+    def _(step):
+        pair = step + first_pair
         columns = tile(pair, LEN)
         for first, rows, count in segments:
             own = pl.ds(first, rows)
@@ -654,72 +654,81 @@
 
 
 class Gather:
-    ORDER = ((0, 1), (2, 3), (4, 5), (6, 7), (12, 13), (14, 15), (8, 9), (10, 11))
+    ORDER = (0, 1, 2, 3, 4, 5, 6, 7, 12, 13, 14, 15, 8, 9, 10, 11)
+    WIDE = ()
+    EARLY = 3
+    ROUTES = {False: ("zxy", "zyx"), True: ("xzy", "yzx")}
+    TIMES = {False: (-3, 0, 1, 2, 3), True: (-20, -3, 1, 2, 3)}
+    SLOTS = 10
 
     def __init__(self, links, moves, own, square, shrink):
         self.links, self.moves, self.own, self.square, self.shrink = links, moves, own, square, shrink
-        self.slots = {unit: links.slot(9) for unit in range(UNITS)}
-        self.local = {unit: moves.start(own(unit), self.block(unit, *self.home())) for unit in range(UNITS)}
-        self.now = 0
-        self.sent_pairs = 0
-
-    def home(self):
-        place = self.links.place
-        return (place.y, place.x, place.z, place.core)
+        self.first_slot = links.slot(UNITS * 2 * self.SLOTS)
+        self.local = {}
+        for unit in self.ORDER:
+            target = self.block(unit, links.place.y, links.place.x, links.place.z, links.place.core)
+            self.local[unit] = moves.start(own(unit), target)
+        self.now = -self.EARLY
+        self.steps = {}
+        for number, unit in enumerate(self.ORDER):
+            wide = number in self.WIDE
+            for half in (0, 1):
+                for phase, time in enumerate(self.TIMES[wide]):
+                    step = (phase, number, unit, half, self.ROUTES[wide][half])
+                    self.steps.setdefault(max(number + time, self.now), []).append(step)
 
     def block(self, unit, *index):
         if unit < SQUARE:
             return self.square.at[(unit,) + index]
-        return self.shrink.at[index + (unit - SQUARE,)]
-
-    def phase(self, unit, number):
-        links, place, slot = self.links, self.links.place, self.slots[unit]
-        y, x, z, core = self.home()
-        by_x = unit % 2 == 0
-        first, second = ("x", "y") if by_x else ("y", "x")
-        line = (y, x, ALL)
-        line_in = (y, 1 - x, ALL) if by_x else (1 - y, x, ALL)
-        sheet = (y, ALL, ALL) if by_x else (ALL, x, ALL)
-        sheet_in = (1 - y, ALL, ALL) if by_x else (ALL, 1 - x, ALL)
-
-        def share(number, index, device):
-            part = self.block(unit, *index, core)
-            links.send(slot + number, part, part, device)
-
-        def arrived(number, index, plane):
-            links.arrived(slot + number, self.block(unit, *index, plane))
-
-        if number == 0:
-            for k in (1, 2, 3):
-                links.send(slot + z, self.own(unit), self.block(unit, y, x, z, core), place.along_z(k))
-        if number == 1:
-            self.moves.wait(self.local[unit])
-            for k in (1, 2, 3):
-                arrived((z + k) % 4, (y, x, (z + k) % 4), core)
-            share(4, line, place.across(first))
-            share(6, line, place.across("core"))
-        if number == 2:
-            arrived(4, line_in, core)
-            share(5, sheet, place.across(second))
-            share(7, line_in, place.across("core"))
-        if number == 3:
-            arrived(5, sheet_in, core)
-            share(8, sheet_in, place.across("core"))
-        if number == 4:
-            arrived(6, line, 1 - core)
-            arrived(7, line_in, 1 - core)
-            arrived(8, sheet_in, 1 - core)
+        return self.shrink.at[index[:4] + (unit - SQUARE,) + index[4:]]
 
     def tick(self):
-        if self.now == 0:
-            steps = [(0, 0), (1, 0)]
-        else:
-            steps = [(self.now + 1, 0)] + [(self.now - number, number) for number in (4, 3, 2, 1)]
-        for pair, number in steps:
-            if 0 <= pair < len(self.ORDER):
-                for unit in self.ORDER[pair]:
-                    self.phase(unit, number)
+        for phase, _, unit, half, route in sorted(self.steps.pop(self.now, ())):
+            self.move(phase, unit, half, route)
         self.now += 1
+
+    def move(self, phase, unit, half, route):
+        links, place = self.links, self.links.place
+        here = {"y": place.y, "x": place.x, "z": place.z}
+        slot = self.first_slot + (2 * unit + half) * self.SLOTS
+        rows = pl.ds(16 * half, 16)
+        turn = route.index("z")
+
+        def part(where, core):
+            return self.block(unit, where["y"], where["x"], where["z"], core, rows)
+
+        def reached(count):
+            return {**here, **{axis: ALL for axis in route[:count]}}
+
+        def incoming(count):
+            axis = route[count]
+            if axis == "z":
+                return reached(count + 1)
+            return {**reached(count), axis: 1 - here[axis]}
+
+        if phase == 1 and unit in self.local:
+            self.moves.wait(self.local.pop(unit))
+        if 1 <= phase <= 3:
+            if phase - 1 == turn:
+                for k in (1, 2, 3):
+                    source = (place.z + k) % 4
+                    links.arrived(slot + source, part({**reached(phase - 1), "z": source}, place.core))
+            else:
+                links.arrived(slot + 3 + phase, part(incoming(phase - 1), place.core))
+        if phase < 3:
+            source = self.own(unit).at[rows] if phase == 0 else part(reached(phase), place.core)
+            target = part(reached(phase), place.core)
+            if phase == turn:
+                for k in (1, 2, 3):
+                    links.send(slot + place.z, source, target, place.along_z(k))
+            else:
+                links.send(slot + 4 + phase, source, target, place.across(route[phase]))
+        if 1 <= phase <= 3 and phase > turn:
+            fresh = part(incoming(phase - 1), place.core)
+            links.send(slot + 6 + phase, fresh, fresh, place.across("core"))
+        if phase == 4:
+            for number in range(turn, 3):
+                links.arrived(slot + 7 + number, part(incoming(number), 1 - place.core))
 
 
 def core_rows(core, count=OWN):
@@ -749,6 +758,7 @@
     "third_grad": ((OWN, D), F32),
     "norm_sums": ((8, D), F32),
     "gains": ((8, D), F32),
+    "final_low": ((OWN, D), BF),
 }
 TURNED_SAVES = {
     "tokens_t": ((16, 32, 2 * OWN), BF),
@@ -770,7 +780,6 @@
     "second_low": ((OWN, D), BF),
     "active": ((OWN, D), BF),
     "sums": ((OWN, D), F32),
-    "final_low": ((OWN, D), BF),
     "cotangent": ((OWN, D), BF),
     "branch_own": ((OWN, D), BF),
     "weights": ((4, D, D), BF),
@@ -779,7 +788,7 @@
     "turned_memory": ((16, 2, 32, MEM), BF),
     "work": ((8, 8, D), F32),
 }
-FORWARD_SENDS, FORWARD_SLOTS, FORWARD_MOVES = 192, 224, 96
+FORWARD_SENDS, FORWARD_SLOTS, FORWARD_MOVES = 320, 384, 96
 
 
 class Refs:
@@ -790,8 +799,8 @@
 
 def forward_kernel(lengths, segments, norms, tokens, memory, out_grad, *refs):
     squares, expand_own, shrink_own = refs[:8], refs[8], refs[9]
-    square, shrink, output = refs[10:13]
-    rest = refs[13:]
+    square, shrink = refs[10:12]
+    rest = refs[12:]
     kept = Refs(FORWARD_SAVES, rest[: len(FORWARD_SAVES)])
     rest = rest[len(FORWARD_SAVES) :]
     turned = Refs(TURNED_SAVES, rest[: len(TURNED_SAVES)])
@@ -822,11 +831,12 @@
     other_mate = (other_seq + 2) % 4 + 4 * group
     slot_far, slot_mate, slot_mate_far, slot_core = links.slot(), links.slot(), links.slot(), links.slot(4)
     home = moves.start(tokens.at[group], stream.at[block_rows(seq)])
+    gather = Gather(links, moves, own, square, shrink)
+    for _ in range(Gather.EARLY):
+        gather.tick()
     links.send(slot_far, tokens.at[1 - group], stream.at[block_rows(seq)], opposite)
     links.send(slot_mate, tokens.at[group], stream.at[block_rows(seq)], mate)
     links.send(slot_core, tokens.at[group], stream.at[block_rows(seq)], partner)
-    gather = Gather(links, moves, own, square, shrink)
-    gather.tick()
     slot_memory, slot_context = links.slot(4), links.slot()
     context_home = moves.start(memory.at[group], held.context.at[z, core])
     for k in (1, 2, 3):
@@ -842,6 +852,8 @@
         return result
 
     held.norm_sums[...] = jnp.zeros_like(held.norm_sums)
+    held.self_logs[...] = jnp.zeros_like(held.self_logs)
+    held.cross_logs[...] = jnp.zeros_like(held.cross_logs)
 
     @loop(OWN // STEP)
     def _(index):
@@ -857,31 +869,34 @@
     def pass_on(number, block):
         links.send(slot_core + number, stream.at[block_rows(block)], stream.at[block_rows(block)], partner)
 
+    gather.tick()
+    next(norm_steps)
+    gather.tick()
+    next(norm_steps)
+    gather.tick()
     links.arrived(slot_far, stream.at[block_rows(far)])
     links.send(slot_mate_far, stream.at[block_rows(far)], stream.at[block_rows(far)], mate)
     pass_on(1, far)
     gather.tick()
-    next(norm_steps)
+    links.arrived(slot_mate, stream.at[block_rows(mate_seq)])
+    pass_on(2, mate_seq)
     moves.wait(context_home)
     for k in (1, 2, 3):
         links.arrived(slot_memory + (z + k) % 4, held.context.at[(z + k) % 4, core])
     links.send(slot_context, held.context.at[:, core], held.context.at[:, core], partner)
-    links.arrived(slot_mate, stream.at[block_rows(mate_seq)])
-    pass_on(2, mate_seq)
+    next(norm_steps)
     gather.tick()
-    next(norm_steps)
+    links.arrived(slot_mate_far, stream.at[block_rows((mate_seq + 4) % 8)])
+    pass_on(3, (mate_seq + 4) % 8)
+    gather.tick()
     cotangent_rows, cotangent_far = block_rows(group), block_rows(1 - group)
     slot_cotangent = links.slot()
     cotangent_home = moves.start(out_grad.at[group], held.cotangent.at[cotangent_rows])
     links.send(slot_cotangent, out_grad.at[1 - group], held.cotangent.at[cotangent_rows], opposite)
-    links.arrived(slot_mate_far, stream.at[block_rows((mate_seq + 4) % 8)])
-    pass_on(3, (mate_seq + 4) % 8)
     moves.wait(home)
     for number, block in enumerate((other_seq, (other_seq + 4) % 8, other_mate, (other_mate + 4) % 8)):
         links.arrived(slot_core + number, stream.at[block_rows(block)])
     links.arrived(slot_context, held.context.at[:, 1 - core])
-    gather.tick()
-    next(norm_steps)
     held.mine[pl.ds(0, LEN), :] = stream[block_rows(low), :]
     held.mine[pl.ds(LEN, LEN), :] = stream[block_rows(low + 4), :]
 
@@ -928,23 +943,31 @@
     def bias(number):
         return held.gains[pl.ds(3 + number, 1), :]
 
-    gather.tick()
     fetch(KEY, 0)
-    fetch(VALUE, 1)
     turn(held.mine, "tokens_t")
     next(norm_steps)
+    fetch(VALUE, 1)
     rows_times(stream, weight(KEY), put(held.keys))
     gather.tick()
     fetch(QUERY, 2)
-    fetch(OUT, 3)
     rows_times(stream, weight(VALUE), put(held.values))
     rows_times(held.mine, weight(QUERY), put(held.queries))
-    attend_rows(held.queries, held.keys, held.values, held.self_bias, held.self_logs, held.attended, SELF_SEGMENTS)
+
+    def attend_part(first, pairs):
+        attend_rows(
+            held.queries, held.keys, held.values, held.self_bias, held.self_logs, held.attended, SELF_SEGMENTS, pairs, first
+        )
+
+    fetch(OUT, 3)
+    attend_part(0, 3)
     gather.tick()
     fetch(CROSS_QUERY, 0)
+    attend_part(3, 3)
+    gather.tick()
     fetch(CROSS_KEY, 1)
+    attend_part(6, 2)
+    rows_times(held.attended, weight(OUT), put(held.sums, F32))
     keep("queries", "keys", "values", "self_bias", "self_logs", "cross_bias", "gains")
-    rows_times(held.attended, weight(OUT), put(held.sums, F32))
 
     def first_rows(rows, result, _):
         held.first_low[rows, :] = (result * gain(0) + bias(0)).astype(BF)
@@ -959,7 +982,6 @@
     rows_times(context, weight(CROSS_KEY), put(held.cross_keys), MEM)
     gather.tick()
     fetch(CROSS_VALUE, 2)
-    fetch(CROSS_OUT, 3)
     turn(held.first_low, "first_t")
 
     @loop(4)
@@ -972,6 +994,8 @@
         held.cross_queries, held.cross_keys, held.cross_values, held.cross_bias, held.cross_logs,
         held.cross_attended, CROSS_SEGMENTS,
     )
+    gather.tick()
+    fetch(CROSS_OUT, 3)
     keep("cross_queries", "cross_keys", "cross_values", "cross_logs", "normal_one", "inverse_one")
     rows_times(held.cross_attended, weight(CROSS_OUT), put(held.sums, F32))
 
@@ -986,15 +1010,14 @@
     gather.tick()
     turn(held.cross_attended, "cross_t")
     turn(held.second_low, "second_t")
-    gather.tick()
+    for _ in range(3):
+        gather.tick()
     held.sums[...] = jnp.zeros_like(held.sums)
     turned_open = {}
     for part in range(4):
-        if part % 2 == 0:
-            gather.tick()
-            for number in (0, 1):
-                fetch(EXPAND + part + number, 2 * number)
-                fetch(SQUARE + part + number, 2 * number + 1)
+        fetch(SQUARE + part, 2 * (part % 2) + 1)
+        gather.tick()
+        fetch(EXPAND + part, 2 * (part % 2))
         expand = weight(EXPAND + part)
         slopes = held.slopes.at[part]
 
@@ -1042,13 +1065,9 @@
     links.send(slot, held.branch_own, turned.branch.at[mine], partner)
     landing.append((slot, turned.branch.at[theirs]))
     moves.start(held.branch_own, turned.branch.at[mine])
-    keep("third_grad", "norm_sums")
-    slot = links.slot()
-    moves.start(held.final_low.at[block_rows(group)], output.at[group])
-    links.send(slot, held.final_low.at[block_rows(1 - group)], output.at[group], opposite)
+    keep("third_grad", "norm_sums", "final_low")
     for arrival in landing:
         links.arrived(*arrival)
-    links.arrived(slot, output.at[1 - group])
     moves.finish()
     links.finish()
 
@@ -1070,7 +1089,6 @@
     results = [
         jax.ShapeDtypeStruct(SQUARE_SHAPE, BF),
         jax.ShapeDtypeStruct(SHRINK_SHAPE, BF),
-        jax.ShapeDtypeStruct(tokens.shape, BF),
         *shapes_of(FORWARD_SAVES),
         *shapes_of(TURNED_SAVES),
     ]
@@ -1088,8 +1106,8 @@
         ],
         compiler_params=pltpu.CompilerParams(collective_id=0, has_side_effects=True, vmem_limit_bytes=VMEM_BYTES),
     )(lengths, segments, norms, tokens, memory, out_grad, *weights)
-    saves = dict(zip([*FORWARD_SAVES, *TURNED_SAVES], values[3:]))
-    return values[0], values[1], values[2], saves
+    saves = dict(zip([*FORWARD_SAVES, *TURNED_SAVES], values[2:]))
+    return values[0], values[1], saves
 
 
 class Scatter:
@@ -1148,7 +1166,7 @@
             self.result(unit, rows, total)
 
     def tick(self):
-        for number in (3, 2, 1, 0):
+        for number in (0, 1, 2, 3):
             unit = self.now - number
             if 0 <= unit < UNITS:
                 for half in (0, 1):
@@ -1187,11 +1205,13 @@
 
 
 def backward_kernel(square, shrink, *refs):
-    names = [*FORWARD_SAVES, *TURNED_SAVES]
-    kept = Refs(names, refs[: len(names)])
-    rest = refs[len(names) :]
-    input_grad, memory_grad, unit_grads, expand_grad, shrink_grad, norm_grads = rest[0], rest[1], rest[2:10], *rest[10:13]
-    rest = rest[13:]
+    saved = [*FORWARD_SAVES, *TURNED_SAVES]
+    names = [name for name in saved if name != "final_low"]
+    kept = Refs(saved, refs[: len(saved)])
+    rest = refs[len(saved) :]
+    output, input_grad, memory_grad, *unit_grads = rest[:11]
+    expand_grad, shrink_grad, norm_grads = rest[11:14]
+    rest = rest[14:]
     held = Refs(names, rest[: len(names)])
     rest = rest[len(names) :]
     held.__dict__.update(Refs(BACKWARD_SCRATCH, rest[: len(BACKWARD_SCRATCH)]).__dict__)
@@ -1276,6 +1296,9 @@
 
     produce_shrink(0)
     scatter.tick()
+    slot_output = links.slot()
+    moves.start(kept.final_low.at[block_rows(group)], output.at[group])
+    links.send(slot_output, kept.final_low.at[block_rows(1 - group)], output.at[group], place.along_z(2))
     for part in (1, 2, 3):
         produce_shrink(part)
     scatter.tick()
@@ -1415,7 +1438,6 @@
 
     produce(lambda: held.memory_t[...], held.cross_sums.at[1], MEM)
     scatter.tick()
-    key_rows = held.cross_sums[0].reshape(4, 2, 16, D)
 
     cross_key, cross_value = weight(CROSS_KEY, 0), weight(CROSS_VALUE, 2)
     sums = held.cross_sums.reshape(2, 4, 2, 16, D)
@@ -1476,22 +1498,25 @@
     input_grad[1 - group] = held.far_in[...].astype(F32)
     scatter.tick()
     scatter.tick()
+    links.arrived(slot_output, output.at[1 - group])
     moves.finish()
     links.finish()
 
 
 def backward_call(square, shrink, saves, block_shape, memory_shape):
-    results = [jax.ShapeDtypeStruct(block_shape, F32), jax.ShapeDtypeStruct(memory_shape, F32)]
+    results = [jax.ShapeDtypeStruct(block_shape, BF)]
+    results += [jax.ShapeDtypeStruct(shape, F32) for shape in (block_shape, memory_shape)]
     results += [jax.ShapeDtypeStruct((32, D), F32)] * 8
     results += [jax.ShapeDtypeStruct(shape, F32) for shape in ((32, 4 * D), (LEN, D), (8, D))]
     saved = {**FORWARD_SAVES, **TURNED_SAVES}
+    held = {name: saved[name] for name in saved if name != "final_low"}
     return pl.pallas_call(
         backward_kernel,
         in_specs=[IN_PLACE] * (2 + len(saved)),
-        out_specs=[IN_VMEM] * len(results),
+        out_specs=[IN_PLACE] + [IN_VMEM] * (len(results) - 1),
         out_shape=results,
         scratch_shapes=[
-            *vmem_of(saved),
+            *vmem_of(held),
             *vmem_of(BACKWARD_SCRATCH),
             pltpu.SemaphoreType.DMA((BACKWARD_SENDS,)),
             pltpu.SemaphoreType.DMA((BACKWARD_SLOTS,)),
@@ -1499,6 +1524,34 @@
         ],
         compiler_params=pltpu.CompilerParams(collective_id=1, has_side_effects=True, vmem_limit_bytes=63 << 20),
     )(square, shrink, *(saves[name] for name in saved))
+
+
+def hand_over_kernel(*refs):
+    count = len(refs) // 3
+    sem = refs[-1]
+    loads = [pltpu.make_async_copy(refs[n], refs[2 * count + n], sem.at[0, n]) for n in range(count)]
+    stores = [pltpu.make_async_copy(refs[2 * count + n], refs[count + n], sem.at[1, n]) for n in range(count)]
+    for load in loads:
+        load.start()
+    for load, store in zip(loads, stores):
+        load.wait()
+        store.start()
+    for store in stores:
+        store.wait()
+
+
+def hand_over(values):
+    return pl.pallas_call(
+        hand_over_kernel,
+        in_specs=[IN_PLACE] * len(values),
+        out_specs=[IN_PLACE] * len(values),
+        out_shape=[jax.ShapeDtypeStruct(value.shape, value.dtype) for value in values],
+        scratch_shapes=[
+            *(pltpu.VMEM(value.shape, value.dtype) for value in values),
+            pltpu.SemaphoreType.DMA((2, len(values))),
+        ],
+        compiler_params=pltpu.CompilerParams(vmem_limit_bytes=VMEM_BYTES),
+    )(*values)
 
 
 def fast_shards(
@@ -1511,11 +1564,11 @@
     norms = jnp.concatenate([norm_gains, norm_biases, jnp.zeros((2, 32), BF)]).astype(F32)
     norms = lax.dynamic_update_slice(jnp.zeros((8, D), F32), norms, (0, 32 * me))
     weights = (self_key, self_value, self_query, self_out, cross_query, cross_key, cross_value, cross_out)
-    square, shrink, output, saves = forward_call(
+    square, shrink, saves = forward_call(
         lengths, memory_segments, norms, tokens, memory, out_grad, (*weights, expand_weight, shrink_weight)
     )
-    values = backward_call(square, shrink, saves, tokens.shape, memory.shape)
-    input_grad, memory_grad, units, expand_grad, shrink_grad, norm_grads = values[0], values[1], values[2:10], *values[10:]
+    *values, norm_grads = backward_call(square, shrink, saves, tokens.shape, memory.shape)
+    output, input_grad, memory_grad, *units, expand_grad, shrink_grad = hand_over(values)
     norm_grads = lax.dynamic_slice(norm_grads, (0, 32 * me), (8, 32))
     return (
         output,

time: 426 us -> 403 us (0.946); the launches traced: 426 us -> 398 us
  Pallas kernels: 411 us -> 394 us
  local copies, waits for them, and re-layouts: 13 us -> 2.23 us
    pallas_call x1, Pallas kernels: 219 us -> 199 us  [forward_call(): pl.pallas_call(forward_kernel, in_specs=[IN_SMEM, IN_VMEM, IN_VMEM] + [IN...]
    unnamed x39 -> x2, local copies, waits for them, and re-layouts: 11.3 us -> 0.61 us
where the time goes in v3:
time: 403 us; the launch traced here: 398 us
  Pallas kernels  394 us (98%)
    pallas_call x1, Pallas kernels, forward_call(): pl.pallas_call(forward_kernel, in_specs=[IN_SMEM, IN_VMEM, IN_VMEM] + [IN...  199 us
    pallas_call x1, Pallas kernels, backward_call(): pl.pallas_call(backward_kernel, in_specs=[IN_PLACE] * (2 + len(saved)), o...  191 us

profile of v3, /device:TPU:0, one launch (start us, length us, event | category | flops | bytes accessed | tf_op | source)
XLA Modules:
  0.0 397.8 jit_solution(928477591686645254)
XLA Ops:
  0.7 0.1 pad.2.clone
  0.7 0.8 maximum_convert_fusion
  1.5 0.2 dynamic_update_slice.3.norms
  1.7 0.0 copy-start
  1.7 0.6 copy-done
  2.3 199.4 %shard_map.280 = (bf16[12,2,2,4,2,32,1024]{6,5,4,3,2,1,0:T(8,128)(2,1)}, bf16[2,2,4,2,4,32,1024]{6,5,4,3,2,1,0:T(8,128)(2,1)}, bf16[256,1024]{1,0:T(8,128)(2,1)}...) custom-call(s32[2,8]{1,0:T(2,128)} %lengths.1, ...), custom_call_target="tpu_custom_call" | custom-call | tf_op jit(solution)/shard_map/pallas_call | solution.py:1095
  201.7 191.2 %shard_map.281 = (bf16[2,128,1024]{2,1,0:T(8,128)(2,1)}, f32[2,128,1024]{2,1,0:T(8,128)}, f32[2,16,1024]{2,1,0:T(8,128)}, f32[32,1024]{1,0:T(8,128)}, f32[32,102...) custom-call(bf16[12,2,2,4,2,32,1024]{6,5,4,3,2,1,0:T(8,128)(2,1)} %g, ...), custom_call_target="tpu_custom_call" | custom-call | tf_op jit(solution)/shard_map/pallas_call | solution.py:1513
  392.9 3.3 shard_map.282
  396.2 0.8 constant_dynamic-slice_fusion
  397.0 0.6 fusion
  (2 shorter events, 0.0 us)
Async XLA Ops:
  1.7 0.6 copy-start
